TPU v7x, 256 devices: a whole 4x4x8 slice. The times are simulated.
256 devices in a mesh: tok: 8 (over z_lo, core), row: 4 (over x), col: 8 (over z_hi, y).
Axes of the slice: x: 4, y: 4, z: 8 (z_hi: 2, z_lo: 4; z = z_hi * 4 + z_lo), core: 2. Of those that a mesh axis runs over, the one named last changes fastest.
Arguments:
- hidden: bfloat16 [4096, 5120], P('tok', ('row', 'col')), may hold values from -6 to 6
- gains: float32 [8, 5120], P('tok', ('row', 'col')), may hold values from 0.25 to 1.75
- weights: bfloat16 [8, 5120, 2048], P('tok', 'row', 'col'), may hold values from -6 to 6
- lengths: int32 [8], replicated, may hold values from 1 to 512, 2304 in all
Outputs:
- merged: float32 [5120, 2048], P(('row', 'tok'), 'col')
Inputs may be any that keep to these rules, and one draw needn't show every extreme that they name: The largest entry of lengths is exactly 512.
All inputs are finite; a program needn't handle non-finite values.
Results may differ from a plain program's by a relative error of at most 0.0054.
Values may be sent and summed in bfloat16 or wider, within the bound.
A program may use at most 64 MiB of HBM per device.

v0:
```python
import jax
import jax.numpy as jnp
from jax import lax
from jax.sharding import PartitionSpec as P

ITERS = 4


MIXING = 0.9
EPSILON = 1e-06


def body(hidden, gains, weights, lengths):
    row_devices = lax.axis_size("row")
    col_devices = lax.axis_size("col")
    tok_devices = lax.axis_size("tok")
    slots, width_dev = hidden.shape
    model_width = width_dev * row_devices * col_devices
    sub_rows = model_width // (row_devices * tok_devices)
    length = lengths[lax.axis_index("tok")]
    values = hidden.astype(jnp.float32)
    squares = lax.psum(jnp.sum(values * values, axis=1), ("row", "col"))
    inverse_rms = lax.rsqrt(squares / model_width + EPSILON)
    live_mask = (jnp.arange(slots, dtype=jnp.int32) < length).astype(jnp.float32)
    normed = (values * (inverse_rms * live_mask)[:, None] * gains[0][None, :]).astype(jnp.bfloat16)
    row_block = lax.all_gather(normed, "col", axis=1, tiled=True)
    gram_term = lax.dot_general(
        lax.all_gather(normed, ("row", "col"), axis=1, tiled=True),
        normed,
        (((0,), (0,)), ((), ())),
        preferred_element_type=jnp.float32,
    )
    gram_term = gram_term.reshape(row_devices, tok_devices, sub_rows, width_dev)
    gram_term = jnp.transpose(gram_term, (1, 0, 2, 3)).reshape(model_width, width_dev)
    gram_share = lax.psum_scatter(gram_term, "tok", scatter_dimension=0, tiled=True)
    operator = lax.all_gather(gram_share, "col", axis=1, tiled=True)
    diag_block = lax.dynamic_slice(
        operator,
        (lax.axis_index("row") * sub_rows, lax.axis_index("tok") * sub_rows),
        (sub_rows, sub_rows),
    )
    diagonal = jnp.diagonal(diag_block)
    w_local = weights[0]
    partial_value = jnp.dot(row_block, w_local, preferred_element_type=jnp.float32)
    outputs = lax.psum(partial_value, "row").astype(jnp.bfloat16)
    squared = jnp.sum(jnp.square(row_block.astype(jnp.float32)), axis=0)
    product = lax.dot_general(
        row_block, outputs, (((0,), (0,)), ((), ())), preferred_element_type=jnp.float32
    )
    weight_rows = w_local.astype(jnp.float32)
    right = lax.psum_scatter(
        MIXING * product + (1.0 - MIXING) * squared[:, None] * weight_rows,
        "tok",
        scatter_dimension=0,
        tiled=True,
    )

    def column_norms(residual):
        return lax.psum(jnp.sum(residual * residual, axis=0), ("tok", "row"))

    merged = jnp.zeros_like(right)
    residual = right
    direction = right
    norm_now = column_norms(residual)
    for step in range(ITERS):
        gathered = lax.all_gather(direction, "row", axis=0, tiled=True)
        operate_product = lax.dot_general(
            operator,
            gathered,
            (((0,), (0,)), ((), ())),
            precision=lax.Precision.HIGHEST,
            preferred_element_type=jnp.float32,
        )
        summed = lax.psum_scatter(operate_product, "tok", scatter_dimension=0, tiled=True)
        image = MIXING * summed + (1.0 - MIXING) * diagonal[:, None] * direction
        curvature = lax.psum(jnp.sum(direction * image, axis=0), ("tok", "row"))
        step_size = norm_now / curvature
        merged = merged + step_size[None, :] * direction
        residual = residual - step_size[None, :] * image
        norm_next = column_norms(residual)
        direction = residual + (norm_next / norm_now)[None, :] * direction
        norm_now = norm_next
    return merged


def solution(mesh):
    return jax.shard_map(
        body,
        mesh=mesh,
        in_specs=(P("tok", ("row", "col")), P("tok", ("row", "col")), P("tok", "row", "col"), P()),
        out_specs=P(("row", "tok"), "col"),
        check_vma=False,
    )
```

profile of v0, /device:TPU:1, one launch (start us, length us, event | category | flops | bytes accessed | tf_op | source)
XLA Modules:
  0.0 1197.3 jit_solution(15011545452934528527)
XLA Ops:
  6.5 1.0 fusion.3
  7.5 106.9 %psum.70 = f32[512]{0:T(512)S(1)} all-reduce(f32[512]{0:T(512)S(1)} %fusion.3), channel_id=1, replica_groups=mesh['tok'=8,'row'=4,'col'=8] {'row','col'}, use_global_device_ids=true, to_apply=%region_1.0 | all-reduce | flops 512 | bytes 4096 | tf_op jit(solution)/shard_map/psum | solution.py:22
  114.4 1.2 dynamic_slice.6
  116.3 1.7 fusion.5
  118.8 126.7 %all-gather.6.cloned.1.call-done = bf16[512,5120]{0,1:T(8,128)(2,1)} async-done(((bf16[512,160]{0,1:T(8,128)(2,1)}), bf16[512,5120]{0,1:T(8,128)(2,1)}) %all-gather.6.cloned.1.call-update) | async-done | bytes 5242896 | tf_op jit(solution)/shard_map/all_gather | solution.py:28
  245.5 4.3 fusion.7
  249.8 4.3 reshape.22
  254.2 7.5 copy.11
  261.7 7.7 reshape.23
  269.4 38.0 %all-gather.4.cloned.1.call-done = bf16[512,1280]{0,1:T(8,128)(2,1)} async-done(((bf16[512,160]{0,1:T(8,128)(2,1)}), bf16[512,1280]{0,1:T(8,128)(2,1)}) %all-gather.4.cloned.1.call-update) | async-done | bytes 1310736 | tf_op jit(solution)/shard_map/all_gather | solution.py:26
  307.4 2.0 fusion.1
  309.8 18.9 %all-reduce.2 = bf16[512,256]{1,0:T(8,128)(2,1)S(1)} all-reduce(f32[512,256]{1,0:T(8,128)S(1)} %fusion.1), channel_id=1, replica_groups=mesh['tok'=8,'row'=4,'col'=8] {'row'}, use_global_device_ids=true, to_apply=%region_2.0 | all-reduce | flops 131072 | bytes 786432 | tf_op jit(solution)/shard_map/psum | solution.py:45
  328.7 1.6 fusion
  330.4 20.9 %reduce-scatter.9.cloned.1.call-done = f32[640,160]{0,1:T(8,128)} async-done(((f32[5120,160]{0,1:T(8,128)}), f32[640,160]{0,1:T(8,128)}) %reduce-scatter.9.cloned.1.call-update) | async-done | bytes 409616 | tf_op jit(solution)/shard_map/reduce_scatter | solution.py:35
  351.4 39.5 %reduce-scatter.7.cloned.1.call-done = f32[160,256]{1,0:T(8,128)} async-done(((f32[1280,256]{1,0:T(8,128)}), f32[160,256]{1,0:T(8,128)}) %reduce-scatter.7.cloned.1.call-update) | async-done | bytes 163856 | tf_op jit(solution)/shard_map/reduce_scatter | solution.py:51
  390.8 12.2 %all_gather.24 = f32[640,256]{1,0:T(8,128)} all-gather(f32[160,256]{1,0:T(8,128)} %reduce-scatter.7.cloned.1.call-done), channel_id=1, replica_groups=mesh['tok'=8,'row'=4,'col'=8] {'row'}, dimensions={0}, use_global_device_ids=true | all-gather | bytes 819200 | tf_op jit(solution)/shard_map/all_gather | solution.py:66
  403.1 85.9 %all-gather.8.cloned.1.call-done = f32[640,1280]{0,1:T(8,128)} async-done(((f32[640,160]{0,1:T(8,128)}), f32[640,1280]{0,1:T(8,128)}) %all-gather.8.cloned.1.call-update) | async-done | bytes 3276816 | tf_op jit(solution)/shard_map/all_gather | solution.py:36
  488.9 6.5 fusion.8
  496.5 1.0 copy.9
  497.5 1.9 gather_fusion
  499.5 26.9 %reduce-scatter.11.cloned.1.call-done = f32[160,256]{1,0:T(8,128)} async-done(((f32[1280,256]{1,0:T(8,128)}), f32[160,256]{1,0:T(8,128)}) %reduce-scatter.11.cloned.1.call-update) | async-done | bytes 163856 | tf_op jit(solution)/shard_map/reduce_scatter | solution.py:74
  526.4 1.1 multiply_reduce_fusion.7
  527.5 67.7 %all-reduce = (f32[256]{0:T(256)S(1)}, f32[256]{0:T(256)S(1)}) all-reduce(f32[256]{0:T(256)S(1)} %get-tuple-element.6, f32[256]{0:T(256)S(1)} %get-tuple-element.5), channel_id=1, replica_groups=mesh['tok'=8,'row'=4,'col'=8] {'tok','row'}, use_global_device_ids=true, to_apply=%region_6.7 | all-reduce | flops 512 | bytes 4096 | tf_op jit(solution)/shard_map/psum | solution.py:59
  595.1 1.1 multiply_reduce_fusion.6
  596.3 67.4 %psum.74 = f32[256]{0:T(256)S(1)} all-reduce(f32[256]{0:T(256)S(1)} %multiply_reduce_fusion.6), channel_id=1, replica_groups=mesh['tok'=8,'row'=4,'col'=8] {'tok','row'}, use_global_device_ids=true, to_apply=%region_12.13 | all-reduce | flops 256 | bytes 2048 | tf_op jit(solution)/shard_map/psum | solution.py:59
  663.6 1.1 multiply_add_fusion.5
  665.4 10.1 all_gather.25
  675.6 4.3 fusion.9
  679.9 44.1 %reduce-scatter.13.cloned.1.call-done = f32[160,256]{1,0:T(8,128)} async-done(((f32[1280,256]{1,0:T(8,128)}), f32[160,256]{1,0:T(8,128)}) %reduce-scatter.13.cloned.1.call-update) | async-done | bytes 163856 | tf_op jit(solution)/shard_map/reduce_scatter | solution.py:74
  724.1 1.1 multiply_reduce_fusion.5
  725.2 67.4 %psum.75 = f32[256]{0:T(256)S(1)} all-reduce(f32[256]{0:T(256)S(1)} %multiply_reduce_fusion.5), channel_id=1, replica_groups=mesh['tok'=8,'row'=4,'col'=8] {'tok','row'}, use_global_device_ids=true, to_apply=%region_15.16 | all-reduce | flops 256 | bytes 2048 | tf_op jit(solution)/shard_map/psum | solution.py:76
  792.6 1.9 multiply_reduce_fusion.4
  794.5 67.4 %psum.76 = f32[256]{0:T(256)S(1)} all-reduce(f32[256]{0:T(256)S(1)} %get-tuple-element.9), channel_id=1, replica_groups=mesh['tok'=8,'row'=4,'col'=8] {'tok','row'}, use_global_device_ids=true, to_apply=%region_17.18 | all-reduce | flops 256 | bytes 2048 | tf_op jit(solution)/shard_map/psum | solution.py:59
  861.8 1.0 multiply_add_fusion.3
  863.5 10.1 all_gather.26
  873.7 4.3 fusion.10
  878.1 44.2 %reduce-scatter.15.cloned.1.call-done = f32[160,256]{1,0:T(8,128)} async-done(((f32[1280,256]{1,0:T(8,128)}), f32[160,256]{1,0:T(8,128)}) %reduce-scatter.15.cloned.1.call-update) | async-done | bytes 163856 | tf_op jit(solution)/shard_map/reduce_scatter | solution.py:74
  922.3 1.1 multiply_reduce_fusion.3
  923.4 67.6 %psum.77 = f32[256]{0:T(256)S(1)} all-reduce(f32[256]{0:T(256)S(1)} %multiply_reduce_fusion.3), channel_id=1, replica_groups=mesh['tok'=8,'row'=4,'col'=8] {'tok','row'}, use_global_device_ids=true, to_apply=%region_20.21 | all-reduce | flops 256 | bytes 2048 | tf_op jit(solution)/shard_map/psum | solution.py:76
  991.0 1.2 multiply_reduce_fusion.2
  992.1 67.4 %psum.78 = f32[256]{0:T(256)S(1)} all-reduce(f32[256]{0:T(256)S(1)} %multiply_reduce_fusion.2), channel_id=1, replica_groups=mesh['tok'=8,'row'=4,'col'=8] {'tok','row'}, use_global_device_ids=true, to_apply=%region_22.23 | all-reduce | flops 256 | bytes 2048 | tf_op jit(solution)/shard_map/psum | solution.py:59
  1059.5 1.2 multiply_add_fusion.1
  1061.4 10.4 all_gather.27
  1071.7 4.3 fusion.11
  1076.1 44.3 %reduce-scatter.17.cloned.1.call-done = f32[160,256]{1,0:T(8,128)} async-done(((f32[1280,256]{1,0:T(8,128)}), f32[160,256]{1,0:T(8,128)}) %reduce-scatter.17.cloned.1.call-update) | async-done | bytes 163856 | tf_op jit(solution)/shard_map/reduce_scatter | solution.py:74
  1120.4 1.1 multiply_reduce_fusion.1
  1121.5 67.5 %psum.79 = f32[256]{0:T(256)S(1)} all-reduce(f32[256]{0:T(256)S(1)} %multiply_reduce_fusion.1), channel_id=1, replica_groups=mesh['tok'=8,'row'=4,'col'=8] {'tok','row'}, use_global_device_ids=true, to_apply=%region_25.26 | all-reduce | flops 256 | bytes 2048 | tf_op jit(solution)/shard_map/psum | solution.py:76
  1189.0 1.8 multiply_add_fusion
  (45 shorter events, 5.2 us)
Async XLA Ops:
  6.5 239.0 %all-gather.6.cloned.1.call-start = ((), (), s32[]{:S(2)}) async-start(), calls=%async_computation.8 | async-start | bytes 5406720 | tf_op jit(solution)/shard_map/all_gather | solution.py:28
  118.0 189.5 %all-gather.4.cloned.1.call-start = ((), (), s32[]{:S(2)}) async-start(), calls=%async_computation.6 | async-start | bytes 1474560 | tf_op jit(solution)/shard_map/all_gather | solution.py:26
  118.7 232.6 %reduce-scatter.9.cloned.1.call-start = ((), (), s32[]{:S(2)}) async-start(), calls=%async_computation.9 | async-start | bytes 3686400 | tf_op jit(solution)/shard_map/reduce_scatter | solution.py:35
  269.4 38.1 %copy-start.6 = (bf16[1,1280,256]{2,1,0:T(8,128)(2,1)S(1)}, bf16[1,1280,256]{2,1,0:T(8,128)(2,1)}, u32[]{:S(2)}) copy-start(bf16[1,1280,256]{2,1,0:T(8,128)(2,1)} %param.6) | copy-start | bytes 1966084
  269.4 121.4 %reduce-scatter.7.cloned.1.call-start = ((), (), s32[]{:S(2)}) async-start(), calls=%async_computation.7 | async-start | bytes 1474560 | tf_op jit(solution)/shard_map/reduce_scatter | solution.py:51
  307.4 2.0 copy-start.4
  330.3 158.6 %all-gather.8.cloned.1.call-start = ((), (), s32[]{:S(2)}) async-start(), calls=%async_computation.10 | async-start | bytes 3686400 | tf_op jit(solution)/shard_map/all_gather | solution.py:36
  351.3 175.0 %reduce-scatter.11.cloned.1.call-start = ((), (), s32[]{:S(2)}) async-start(), calls=%async_computation.11 | async-start | bytes 1474560 | tf_op jit(solution)/shard_map/reduce_scatter | solution.py:74
  488.9 6.8 copy-start
  495.5 228.6 %reduce-scatter.13.cloned.1.call-start = ((), (), s32[]{:S(2)}) async-start(), calls=%async_computation.12 | async-start | bytes 1474560 | tf_op jit(solution)/shard_map/reduce_scatter | solution.py:74
  664.7 0.7 copy-start.3
  675.6 117.0 %copy-start.1 = (f32[160,256]{1,0:T(8,128)S(1)}, f32[160,256]{1,0:T(8,128)}, u32[]{:S(2)}) copy-start(f32[160,256]{1,0:T(8,128)} %reduce-scatter.7.cloned.1.call-done) | copy-start | bytes 491524
  679.9 242.4 %reduce-scatter.15.cloned.1.call-start = ((), (), s32[]{:S(2)}) async-start(), calls=%async_computation.13 | async-start | bytes 1474560 | tf_op jit(solution)/shard_map/reduce_scatter | solution.py:74
  862.9 0.7 copy-start.2
  878.0 242.4 %reduce-scatter.17.cloned.1.call-start = ((), (), s32[]{:S(2)}) async-start(), calls=%async_computation.14 | async-start | bytes 1474560 | tf_op jit(solution)/shard_map/reduce_scatter | solution.py:74
  1060.7 0.7 copy-start.5
Sparse Core Ops, SparseCore 0:
  118.1 127.3 all-gather.5
  248.1 59.2 all-gather.3
  310.0 41.2 reduce-scatter.8
  353.9 36.9 reduce-scatter.6
  393.6 95.2 all-gather.7
  495.6 30.7 reduce-scatter.10
  680.0 44.0 reduce-scatter.12
  878.1 44.0 reduce-scatter.14
  1076.2 44.1 reduce-scatter.16
where the time goes:
time: 1200 us
  blocking collectives  641 us (53%)
  waiting for transfers between devices  471 us (39%)
  matrix products  27.3 us (2%)
  local copies, waits for them, and re-layouts  26.5 us (2%)
  other arithmetic  17.3 us (1%)
  between operations  13.3 us (1%)
    psum x4, blocking collectives, column_norms(): return lax.psum(jnp.sum(residual * residual, axis=0), ('tok', 'row'))  270 us
    psum x3, blocking collectives, body(): curvature = lax.psum(jnp.sum(direction * image, axis=0), ('tok', 'row'))  202 us
    reduce_scatter x4, waiting for transfers between devices, body(): lax.psum_scatter(operate_product, 'tok', scatter_dimension=0, tiled=True)  160 us
    all_gather x1, waiting for transfers between devices, body(): lax.all_gather(normed, ('row', 'col'), axis=1, tiled=True)  127 us
    psum x1, blocking collectives, body(): squares = lax.psum(jnp.sum(values * values, axis=1), ('row', 'col'))  107 us
    all_gather x1, waiting for transfers between devices, body(): operator = lax.all_gather(gram_share, 'col', axis=1, tiled=True)  85.9 us
    all_gather x4, blocking collectives, body(): gathered = lax.all_gather(direction, 'row', axis=0, tiled=True)  42.9 us
    reduce_scatter x1, waiting for transfers between devices, body(): lax.psum_scatter(MIXING * product + (1.0 - MIXING) * squared[:, None] * w...  39.5 us
  transfers between devices with their start and end apart: 9, of which 9 were waited for; matrix products, arithmetic and copies ran while one was open for 3% of the time, Pallas kernels for 0%

commit v1 on v0

v1 whole, which is shorter than its diff:
```python
import functools

import jax
import jax.numpy as jnp
from jax import lax
from jax.experimental import pallas as pl
from jax.experimental.pallas import tpu as pltpu
from jax.sharding import PartitionSpec as P

MESH = pl.DeviceIdType.MESH
F32, BF16 = jnp.float32, jnp.bfloat16
WIDTH = 5120
EPSILON = 1e-06
MIXING = 0.9
ITERS = 4
MODELS = 8
QUART = 640
LANES = 2 * QUART
CHUNK = 256
COLS = 16


def dot(a, b):
    return jnp.dot(a, b, preferred_element_type=F32)


def dot_nt(a, b):
    return lax.dot_general(a, b, (((1,), (1,)), ((), ())), preferred_element_type=F32)


def place():
    t = lax.axis_index("tok")
    x = lax.axis_index("row")
    c = lax.axis_index("col")
    return t, x, c


class Copies:
    def __init__(self, send, recv):
        self.send, self.recv, self.n = send, recv, 0

    def start(self, src, dst, device):
        copy = pltpu.make_async_remote_copy(
            src_ref=src,
            dst_ref=dst,
            send_sem=self.send.at[self.n],
            recv_sem=self.recv.at[self.n],
            device_id=device,
            device_id_type=MESH,
        )
        self.n += 1
        copy.start()
        return copy


def prepare_kernel(h_ref, g_ref, len_ref, out_ref, sums, halves, pieces, sq_send, sq_recv, send, recv):
    t, x, c = place()
    core, zl = lax.rem(t, 2), lax.div(t, 2)
    me = x * 8 + c

    def block(k):
        other = lax.rem(me + k, 32)
        return {"row": lax.div(other, 8), "col": lax.rem(other, 8)}

    def line(k):
        return {"tok": lax.rem(zl + k, 4) * 2 + core}

    sibling = {"tok": zl * 2 + 1 - core}
    barrier = pltpu.get_barrier_semaphore()

    def greet(k, _):
        pl.semaphore_signal(barrier, inc=1, device_id=block(k), device_id_type=MESH)
        return 0

    lax.fori_loop(1, 32, greet, 0)
    for k in range(1, 4):
        pl.semaphore_signal(barrier, inc=1, device_id=line(k), device_id_type=MESH)
    pl.semaphore_signal(barrier, inc=1, device_id=sibling, device_id_type=MESH)

    h = h_ref[...].astype(F32)
    squares = jnp.sum(h * h, axis=0, keepdims=True)
    sums[me] = jnp.zeros((8, 128), F32)
    for k in range(4):
        sums[me, k : k + 1, :] = squares[:, 128 * k : 128 * k + 128]
    pl.semaphore_wait(barrier, 35)

    def sums_copy(k):
        return pltpu.make_async_remote_copy(
            src_ref=sums.at[me],
            dst_ref=sums.at[me],
            send_sem=sq_send.at[k],
            recv_sem=sq_recv.at[k],
            device_id=block(k),
            device_id_type=MESH,
        )

    def send_sums(k, _):
        sums_copy(k).start()
        return 0

    def wait_sums(k, _):
        sums_copy(k).wait()
        return 0

    lax.fori_loop(1, 32, send_sums, 0)
    lax.fori_loop(1, 32, wait_sums, 0)
    total = jnp.sum(sums[...], axis=0)
    inverse = lax.rsqrt(total / WIDTH + EPSILON)
    inverse = jnp.concatenate([inverse[k : k + 1] for k in range(4)], axis=1)
    slot = lax.broadcasted_iota(jnp.int32, (1, 512), 1)
    live = (slot < len_ref[t]).astype(F32)
    normed = (h * (inverse * live) * g_ref[...]).astype(BF16)
    halves[0] = normed[:80]
    halves[1] = normed[80:]

    copies = Copies(send, recv)
    mine = lax.div(zl, 2)
    moved = []
    for k in range(1, 4):
        target = lax.rem(zl + k, 4)
        moved.append(copies.start(halves.at[lax.div(target, 2)], pieces.at[t], line(k)))
    pieces[t] = halves[mine]
    handed = [copies.start(pieces.at[t], pieces.at[t], sibling)]
    for k in range(1, 4):
        moved[k - 1].wait_recv()
        model = lax.rem(zl + 4 - k, 4) * 2 + core
        handed.append(copies.start(pieces.at[model], pieces.at[model], sibling))
    for copy in handed:
        copy.wait_recv()

    window = lax.rem(t, 4) * QUART
    source = lax.broadcasted_iota(jnp.int32, (512, QUART), 0)
    shift = source - lax.broadcasted_iota(jnp.int32, (512, QUART), 1)

    def add_model(m, carry):
        acc, first = carry
        size = len_ref[m]
        pick = jnp.where((shift == window - first) & (source < size), 1.0, 0.0).astype(BF16)
        return acc + dot(pieces[m], pick), first + size

    acc, _ = lax.fori_loop(0, MODELS, add_model, (jnp.zeros((80, QUART), F32), jnp.int32(0)))
    out_ref[...] = acc.astype(BF16).reshape(5, 16, QUART)
    for copy in moved + handed:
        copy.wait_send()


def prepare(hidden_t, gains_t, lengths):
    return pl.pallas_call(
        prepare_kernel,
        out_shape=jax.ShapeDtypeStruct((5, 16, QUART), BF16),
        in_specs=[
            pl.BlockSpec(memory_space=pltpu.VMEM),
            pl.BlockSpec(memory_space=pltpu.VMEM),
            pl.BlockSpec(memory_space=pltpu.SMEM),
        ],
        out_specs=pl.BlockSpec(memory_space=pltpu.VMEM),
        scratch_shapes=[
            pltpu.VMEM((32, 8, 128), F32),
            pltpu.VMEM((2, 80, 512), BF16),
            pltpu.VMEM((MODELS, 80, 512), BF16),
            pltpu.SemaphoreType.DMA((32,)),
            pltpu.SemaphoreType.DMA((32,)),
            pltpu.SemaphoreType.DMA((7,)),
            pltpu.SemaphoreType.DMA((7,)),
        ],
        compiler_params=pltpu.CompilerParams(
            collective_id=0, has_side_effects=True, vmem_limit_bytes=32 * 2**20
        ),
    )(hidden_t, gains_t, lengths)


def gather(n_ref, copies, t, x, c, later):
    core = lax.rem(t, 2)
    y, z = lax.rem(c, 4), lax.div(c, 4) * 4 + lax.div(t, 2)

    def at_x(k):
        return {"row": lax.rem(x + k + 4, 4)}

    def at_y(k):
        return {"col": lax.div(c, 4) * 4 + lax.rem(y + k + 4, 4)}

    def at_z(k):
        zz = lax.rem(z + k + 8, 8)
        return {"tok": lax.rem(zz, 4) * 2 + core, "col": lax.div(zz, 4) * 4 + y}

    def zpos(k):
        zz = lax.rem(z + k + 8, 8)
        lanes = pl.ds(pl.multiple_of(lax.rem(zz, 2) * QUART, 128), QUART)
        return lax.div(zz, 4), lax.rem(lax.div(zz, 2), 2), lanes

    def go(ref, device):
        return copies.start(ref, ref, device)

    zh, half, lanes = zpos(0)
    every = slice(None)
    rows_a, rows_b, rows_c = pl.ds(0, 1), pl.ds(1, 2), pl.ds(3, 2)

    own_b = n_ref.at[x, zh, y, half, rows_b, every, lanes]
    own_c = n_ref.at[x, zh, y, half, rows_c, every, lanes]
    own_a = n_ref.at[x, zh, y, half, rows_a, every, lanes]
    b1 = [go(own_b, at_y(k)) for k in (1, -1, 2)]
    c1 = [go(own_c, at_z(k)) for k in (1, -1, 2, -2, 3, -3, 4)]
    a1 = [go(own_a, at_x(k)) for k in (1, -1, 2)]

    def b2(k, part):
        h, f, l = zpos(k)
        return n_ref.at[x, h, pl.ds(2 * part, 2), f, rows_b, every, l]

    def c2(k, part):
        return n_ref.at[lax.rem(x + k + 4, 4), part, y, every, rows_c, every, every]

    for copy in b1:
        copy.wait_recv()
    right = [[go(b2(0, p), at_z(1)) for p in (0, 1)]]
    left = [[go(b2(0, p), at_z(-1)) for p in (1, 0)][::-1]]
    for copy in c1:
        copy.wait_recv()
    c_right = [go(c2(0, p), at_x(1)) for p in (0, 1)]
    c_left = [go(c2(0, p), at_x(-1)) for p in (1, 0)][::-1]
    for copy in a1:
        copy.wait_recv()
    own_a = n_ref.at[every, zh, y, half, rows_a, every, lanes]
    a2 = [go(own_a, at_y(k)) for k in (1, -1, 2)]
    for step in (1, 2):
        r, l = [], []
        for p in (0, 1):
            right[step - 1][p].wait_recv()
            r.append(go(b2(-step, p), at_z(1)))
            left[step - 1][1 - p].wait_recv()
            l.append(go(b2(step, 1 - p), at_z(-1)))
        right.append(r)
        left.append(l[::-1])
        if step == 1:
            c_right[0].wait_recv()
            c_far = [go(c2(-1, 0), at_x(1))]
            c_left[1].wait_recv()
            c_far.append(go(c2(1, 1), at_x(-1)))
    right[2][0].wait_recv()
    b_far = [go(b2(-3, 0), at_z(1))]
    left[2][1].wait_recv()
    b_far.append(go(b2(3, 1), at_z(-1)))
    c_right[1].wait_recv()
    c_left[0].wait_recv()
    for copy in c_far:
        copy.wait_recv()

    def c3(k, part):
        return n_ref.at[every, part, lax.rem(y + k + 4, 4), every, rows_c, every, every]

    def b3(k, part):
        return n_ref.at[lax.rem(x + k + 4, 4), part, every, every, rows_b, every, every]

    def a3(k, part):
        h, f, l = zpos(k)
        return n_ref.at[pl.ds(2 * part, 2), h, every, f, rows_a, every, l]

    c3_right = [go(c3(0, p), at_y(1)) for p in (0, 1)]
    c3_left = [go(c3(0, p), at_y(-1)) for p in (1, 0)][::-1]
    right[2][1].wait_recv()
    left[2][0].wait_recv()
    for copy in b_far:
        copy.wait_recv()
    b3_right = [go(b3(0, p), at_x(1)) for p in (0, 1)]
    b3_left = [go(b3(0, p), at_x(-1)) for p in (1, 0)][::-1]
    for copy in a2:
        copy.wait_recv()
    a_right = [[go(a3(0, p), at_z(1)) for p in (0, 1)]]
    a_left = [[go(a3(0, p), at_z(-1)) for p in (1, 0)][::-1]]
    far = []

    def a_step(step):
        r, l = [], []
        for p in (0, 1):
            a_right[step - 1][p].wait_recv()
            r.append(go(a3(-step, p), at_z(1)))
            a_left[step - 1][1 - p].wait_recv()
            l.append(go(a3(step, 1 - p), at_z(-1)))
        a_right.append(r)
        a_left.append(l[::-1])

    later()
    a_step(1)
    c3_right[0].wait_recv()
    far.append(go(c3(-1, 0), at_y(1)))
    c3_left[1].wait_recv()
    far.append(go(c3(1, 1), at_y(-1)))
    b3_right[0].wait_recv()
    far.append(go(b3(-1, 0), at_x(1)))
    b3_left[1].wait_recv()
    far.append(go(b3(1, 1), at_x(-1)))
    a_step(2)
    a_right[2][0].wait_recv()
    far.append(go(a3(-3, 0), at_z(1)))
    a_left[2][1].wait_recv()
    far.append(go(a3(3, 1), at_z(-1)))
    for copy in (a_right[2][1], a_left[2][0], c3_right[1], c3_left[0], b3_right[1], b3_left[0]):
        copy.wait_recv()
    for copy in far:
        copy.wait_recv()
    sent = b1 + c1 + a1 + a2 + c_right + c_left + c_far + b_far + c3_right + c3_left
    sent += b3_right + b3_left + far
    for pairs in (right, left, a_right, a_left):
        for pair in pairs:
            sent += pair
    return sent


def split(v):
    high = v.astype(BF16)
    low = (v - high.astype(F32)).astype(BF16)
    return jnp.concatenate([high, low], axis=0)


def fold(v):
    return v[:COLS] + v[COLS:]


def solve_kernel(
    piece_ref, w_ref, len_ref, out_ref,
    n_ref, wbuf, d2, image, sq, other, other_sq, norm, other_norm, direction, residual, merged, blocks, landed,
    send, recv,
):
    t, x, c = place()
    core, zl = lax.rem(t, 2), lax.div(t, 2)
    zh, y = lax.div(c, 4), lax.rem(c, 4)
    chip = x * 4 + zl
    sibling = {"tok": zl * 2 + 1 - core}

    def plane(k):
        target = lax.rem(chip + k, 16)
        return {"row": lax.div(target, 4), "tok": lax.rem(target, 4) * 2 + core}

    barrier = pltpu.get_barrier_semaphore()

    def greet(k, _):
        pl.semaphore_signal(barrier, inc=1, device_id=plane(k), device_id_type=MESH)
        return 0

    lax.fori_loop(1, 16, greet, 0)
    for k in (1, 2, 3):
        pl.semaphore_signal(
            barrier, inc=1, device_id={"col": zh * 4 + lax.rem(y + k, 4)}, device_id_type=MESH
        )
    for k in range(4):
        pl.semaphore_signal(
            barrier, inc=1, device_id={"tok": k * 2 + core, "col": (1 - zh) * 4 + y}, device_id_type=MESH
        )
    pl.semaphore_signal(barrier, inc=1, device_id=sibling, device_id_type=MESH)

    lanes = pl.ds(pl.multiple_of(lax.rem(zl, 2) * QUART, 128), QUART)
    n_ref[x, zh, y, lax.div(zl, 2), :, :, lanes] = piece_ref[...]
    pl.semaphore_wait(barrier, 23)

    copies = Copies(send, recv)

    def w_lanes(k):
        return pl.ds(pl.multiple_of(lax.rem(lax.div(chip + 16 - k, 4), 4) * 1280, 128), 1280)

    def w_slot(k):
        return wbuf.at[lax.rem(chip + 16 - k, 4) * 2 + core, :, w_lanes(k)]

    w_moved = []
    for k in range(1, 16):
        w_moved.append(copies.start(w_ref.at[lax.rem(chip + k, 16)], w_slot(0), plane(k)))
    wbuf[t, :, w_lanes(0)] = w_ref[chip]
    w_handed = [copies.start(w_slot(0), w_slot(0), sibling)]

    def hand_weights():
        for k in range(1, 16):
            w_moved[k - 1].wait_recv()
            w_handed.append(copies.start(w_slot(k), w_slot(k), sibling))

    sent = gather(n_ref, copies, t, x, c, hand_weights)
    for copy in w_handed:
        copy.wait_recv()

    def block_of(xx, offset):
        return n_ref[xx, :, :, :, :, :, pl.ds(offset, CHUNK)].reshape(1280, CHUNK)

    def features(xx):
        return slice(xx * 1280, xx * 1280 + 1280)

    image[...] = jnp.zeros_like(image)
    sq[...] = jnp.zeros_like(sq)

    def right_chunk(step, _):
        offset = pl.multiple_of(step * CHUNK, CHUNK)
        lane = lax.broadcasted_iota(jnp.int32, (1, CHUNK), 1) + offset
        slot = lane + core * QUART + jnp.where(lane >= QUART, QUART, 0)
        product = jnp.zeros((MODELS * COLS, CHUNK), F32)
        for xx in range(4):
            weights = wbuf[:, :, features(xx)].reshape(MODELS * COLS, 1280)
            product = product + dot(weights, block_of(xx, offset))
        outputs = jnp.zeros((COLS, CHUNK), F32)
        first = jnp.int32(0)
        masks = []
        for m in range(MODELS):
            size = len_ref[m]
            mask = jnp.where((slot >= first) & (slot < first + size), 1.0, 0.0)
            first = first + size
            masks.append(mask)
            outputs = outputs + mask * product[COLS * m : COLS * m + COLS]
        outputs = outputs.astype(BF16)
        masks = jnp.concatenate(masks, axis=0).astype(BF16)
        for xx in range(4):
            block = block_of(xx, offset)
            image[:, features(xx)] += dot_nt(outputs, block)
            sq[:, features(xx)] += dot_nt(masks, block * block)
        return 0

    lax.fori_loop(0, LANES // CHUNK, right_chunk, 0)
    swap = [
        copies.start(image, other.at[0], sibling),
        copies.start(sq, other_sq, sibling),
    ]
    swap[0].wait_recv()
    swap[1].wait_recv()
    squared = sq[...] + other_sq[...]
    right = MIXING * (image[...] + other[0])
    for m in range(MODELS):
        right = right + (1.0 - MIXING) * squared[m : m + 1] * wbuf[m].astype(F32)
    diagonal = (1.0 - MIXING) * jnp.sum(squared, axis=0, keepdims=True)
    direction[...] = right
    residual[...] = right
    norm_now = jnp.sum(right * right, axis=1, keepdims=True)
    swap[0].wait_send()
    swap[1].wait_send()

    def project(offset):
        total = jnp.zeros((2 * COLS, CHUNK), F32)
        for xx in range(4):
            total = total + dot(d2[:, features(xx)], block_of(xx, offset))
        return fold(total)

    def image_chunk(step, _):
        offset = pl.multiple_of(step * CHUNK, CHUNK)
        both = split(project(offset))
        for xx in range(4):
            image[:, features(xx)] += fold(dot_nt(both, block_of(xx, offset)))
        return 0

    def norm_chunk(step, total):
        part = project(pl.multiple_of(step * CHUNK, CHUNK))
        part = part * part
        return total + part[:, :128] + part[:, 128:]

    for step in range(ITERS):
        d2[...] = split(direction[...])
        if step < ITERS - 1:
            image[...] = jnp.zeros_like(image)
            lax.fori_loop(0, LANES // CHUNK, image_chunk, 0)
            swap = copies.start(image, other.at[step + 1], sibling)
            swap.wait_recv()
            now = direction[...]
            full = MIXING * (image[...] + other[step + 1]) + diagonal * now
            curvature = jnp.sum(now * full, axis=1, keepdims=True)
            step_size = norm_now / curvature
            rest = residual[...] - step_size * full
            residual[...] = rest
            norm_next = jnp.sum(rest * rest, axis=1, keepdims=True)
            if step == 0:
                merged[...] = step_size * now
            else:
                merged[...] += step_size * now
            direction[...] = rest + (norm_next / norm_now) * now
            norm_now = norm_next
            swap.wait_send()
        else:
            norm[...] = lax.fori_loop(0, LANES // CHUNK, norm_chunk, jnp.zeros((COLS, 128), F32))
            swap = copies.start(norm, other_norm, sibling)
            swap.wait_recv()
            now = direction[...]
            inner = jnp.sum(norm[...] + other_norm[...], axis=1, keepdims=True)
            curvature = MIXING * inner + jnp.sum(diagonal * now * now, axis=1, keepdims=True)
            result = merged[...] + (norm_now / curvature) * now
            swap.wait_send()

    blocks[...] = jnp.zeros_like(blocks)
    for b in range(32):
        blocks[b, :, 0:160] = result[:, 160 * b : 160 * b + 160]
    landed[chip] = blocks[x * 8 + t]
    moved = []
    for k in range(1, 16):
        target = lax.rem(chip + k, 16)
        target = lax.div(target, 4) * 8 + lax.rem(target, 4) * 2 + core
        moved.append(copies.start(blocks.at[target], landed.at[chip], plane(k)))
    for copy in moved:
        copy.wait_recv()
    out_ref[...] = landed[...].reshape(256, 256)
    for copy in sent + w_moved + w_handed + moved:
        copy.wait_send()


def solve(piece, weights_t, lengths):
    vmem = pl.BlockSpec(memory_space=pltpu.VMEM)
    wide = (COLS, WIDTH)
    count = 160
    return pl.pallas_call(
        solve_kernel,
        out_shape=jax.ShapeDtypeStruct((256, 256), F32),
        in_specs=[vmem, vmem, pl.BlockSpec(memory_space=pltpu.SMEM)],
        out_specs=vmem,
        scratch_shapes=[
            pltpu.VMEM((4, 2, 4, 2, 5, 16, LANES), BF16),
            pltpu.VMEM((MODELS, COLS, WIDTH), BF16),
            pltpu.VMEM((2 * COLS, WIDTH), BF16),
            pltpu.VMEM(wide, F32),
            pltpu.VMEM((MODELS, WIDTH), F32),
            pltpu.VMEM((ITERS, COLS, WIDTH), F32),
            pltpu.VMEM((MODELS, WIDTH), F32),
            pltpu.VMEM((COLS, 128), F32),
            pltpu.VMEM((COLS, 128), F32),
            pltpu.VMEM(wide, F32),
            pltpu.VMEM(wide, F32),
            pltpu.VMEM(wide, F32),
            pltpu.VMEM((32, COLS, 256), F32),
            pltpu.VMEM((16, COLS, 256), F32),
            pltpu.SemaphoreType.DMA((count,)),
            pltpu.SemaphoreType.DMA((count,)),
        ],
        compiler_params=pltpu.CompilerParams(
            collective_id=1, has_side_effects=True, vmem_limit_bytes=56 * 2**20
        ),
    )(piece, weights_t, lengths)


def body(hidden, gains, weights, lengths):
    piece = prepare(hidden.T, gains.T, lengths)
    merged = solve(piece, weights[0].T.reshape(16, COLS, 1280), lengths)
    return merged[:, :160].T


def solution(mesh):
    return jax.shard_map(
        body,
        mesh=mesh,
        in_specs=(P("tok", ("row", "col")), P("tok", ("row", "col")), P("tok", "row", "col"), P()),
        out_specs=P(("row", "tok"), "col"),
        check_vma=False,
    )
```

time: 1200 us -> 189 us (0.16)
  blocking collectives: 641 us -> 0 us
  waiting for transfers between devices: 471 us -> 0 us
  Pallas kernels: 0 us -> 182 us
  matrix products: 27.3 us -> 0 us
  local copies, waits for them, and re-layouts: 26.5 us -> 6.78 us
  other arithmetic: 17.3 us -> 0 us
  between operations: 13.3 us -> 0.04 us
    psum x9 -> x0, blocking collectives: 598 us -> none  [the longest x4 270 us: column_norms(): return lax.psum(jnp.sum(residual * residual, axis=0), ('tok', 'row'))]
    all_gather x3 -> x0, waiting for transfers between devices: 251 us -> none  [the longest x1 127 us: body(): lax.all_gather(normed, ('row', 'col'), axis=1, tiled=True)]
    reduce_scatter x6 -> x0, waiting for transfers between devices: 220 us -> none  [the longest x4 160 us: body(): lax.psum_scatter(operate_product, 'tok', scatter_dimension=0, tiled=True)]
    pallas_call x0 -> x2, Pallas kernels: none -> 182 us  [the longest x1 152 us: solve(): pl.pallas_call(solve_kernel, out_shape=jax.ShapeDtypeStruct((256, 256), F...]
    all_gather x4 -> x0, blocking collectives: 42.9 us -> none  [body(): gathered = lax.all_gather(direction, 'row', axis=0, tiled=True)]
    dot_general x7 -> x0, matrix products: 27.3 us -> none  [the longest x4 19.4 us: body(): lax.dot_general(operator, gathered, (((0,), (0,)), ((), ())), precision=l...]
    reshape x3 -> x0, local copies, waits for them, and re-layouts: 19.5 us -> none  [the longest x2 11.8 us: body(): gram_term = gram_term.reshape(row_devices, tok_devices, sub_rows, width_dev)]
  transfers between devices with their start and end apart: 9 -> 0, of which waited for: 9 -> 0; matrix products, arithmetic and copies ran while one was open for 3% -> 0% of each run, Pallas kernels for 0% -> 0%
where the time goes in v1:
time: 189 us; the launch traced here: 188 us
  Pallas kernels  182 us (96%)
  local copies, waits for them, and re-layouts  6.78 us (4%)
    pallas_call x1, Pallas kernels, solve(): pl.pallas_call(solve_kernel, out_shape=jax.ShapeDtypeStruct((256, 256), F...  152 us
    pallas_call x1, Pallas kernels, prepare(): pl.pallas_call(prepare_kernel, out_shape=jax.ShapeDtypeStruct((5, 16, QUA...  29.8 us

profile of v1, /device:TPU:1, one launch (start us, length us, event | category | flops | bytes accessed | tf_op | source)
XLA Modules:
  0.0 188.3 jit_solution(465345527063074448)
XLA Ops:
  0.0 0.0 copy-start.3
  0.0 0.7 copy-done.3
  0.7 0.0 copy-start.2
  0.7 0.1 copy.7.g_ref
  0.8 0.5 copy-done.2
  1.3 0.0 copy-start.1
  1.3 0.9 copy-done.1
  2.3 29.8 %shard_map.46.piece_ref = bf16[5,16,640]{2,1,0:T(8,128)(2,1)S(1)} custom-call(bf16[160,512]{1,0:T(8,128)(2,1)S(1)} %bitcast.8, f32[160,1]{1,0:T(8,128)S(1)} %copy.7.g_ref, s32[8]{0:T(128)S(1)} %copy-done.2), custom_call_target="tpu_custom_call" | custom-call | tf_op jit(solution)/shard_map/pallas_call | solution.py:148
  32.1 0.0 copy-start
  32.1 0.6 copy-done
  32.7 2.2 %copy.8 = bf16[256,1280]{1,0:T(8,128)(2,1)} copy(bf16[256,1280]{0,1:T(8,128)(2,1)} %bitcast.10) | data formatting | bytes 1310720 | tf_op jit(solution)/shard_map/transpose | solution.py:529
  34.9 151.7 %shard_map.47 = f32[256,256]{1,0:T(8,128)} custom-call(bf16[5,16,640]{2,1,0:T(8,128)(2,1)} %copy-done, bf16[16,16,1280]{2,1,0:T(8,128)(2,1)} %bitcast.9, s32[8]{0:T(128)} %len_ref.3), custom_call_target="tpu_custom_call" | custom-call | tf_op jit(solution)/shard_map/pallas_call | solution.py:498
  186.6 1.0 slice_bitcast_fusion
  187.6 0.8 copy.9
Async XLA Ops:
  0.0 0.7 copy-start.3
  0.7 0.7 copy-start.2
  1.3 0.9 copy-start.1
  32.1 0.6 copy-start

commit v2 on v0

v2 whole, which is shorter than its diff:
```python
import functools

import jax
import jax.numpy as jnp
from jax import lax
from jax.experimental import pallas as pl
from jax.experimental.pallas import tpu as pltpu
from jax.sharding import PartitionSpec as P

MESH = pl.DeviceIdType.MESH
F32, BF16 = jnp.float32, jnp.bfloat16
WIDTH = 5120
EPSILON = 1e-06
MIXING = 0.9
ITERS = 4
MODELS = 8
QUART = 640
LANES = 2 * QUART
CHUNK = 256
COLS = 16


def dot(a, b):
    return jnp.dot(a, b, preferred_element_type=F32)


def dot_nt(a, b):
    return lax.dot_general(a, b, (((1,), (1,)), ((), ())), preferred_element_type=F32)


def place():
    t = lax.axis_index("tok")
    x = lax.axis_index("row")
    c = lax.axis_index("col")
    return t, x, c


class Copies:
    def __init__(self, send, recv):
        self.send, self.recv, self.n = send, recv, 0

    def start(self, src, dst, device):
        copy = pltpu.make_async_remote_copy(
            src_ref=src,
            dst_ref=dst,
            send_sem=self.send.at[self.n],
            recv_sem=self.recv.at[self.n],
            device_id=device,
            device_id_type=MESH,
        )
        self.n += 1
        copy.start()
        return copy


class Plan:
    RATE, HOP = 45e3, 2.3

    def __init__(self):
        self.tasks = []

    def add(self, ref, device, link, size, deps, hops=1):
        self.tasks.append((ref, device, link, size, tuple(deps), hops))
        return len(self.tasks) - 1

    def ring(self, ref, device, axis, n, size, deps, way):
        deps = list(deps)
        right = [self.add(ref(0), device(1), axis + "+", size, deps)]
        left = [self.add(ref(0), device(-1), axis + "-", size, deps)]
        for k in range(1, n // 2 - 1):
            right.append(self.add(ref(-k), device(1), axis + "+", size, right[-1:]))
            left.append(self.add(ref(k), device(-1), axis + "-", size, left[-1:]))
        last = n // 2 - 1
        if way == 0:
            far = self.add(ref(-last), device(1), axis + "+", size, right[-1:])
        else:
            far = self.add(ref(last), device(-1), axis + "-", size, left[-1:])
        arrived = {0: deps, n // 2: [far]}
        for k in range(1, n // 2):
            arrived[-k] = [right[k - 1]]
            arrived[k] = [left[k - 1]]
        return arrived

    def straight(self, ref, device, axis, n, size, deps):
        arrived = {0: list(deps)}
        for k in sorted(range(1 - n // 2, n // 2 + 1), key=abs):
            if k:
                link = axis + ("-" if k < 0 else "+")
                one = self.add(ref(0), device(k), link, size * abs(k), deps, abs(k))
                arrived[k if k == n // 2 else -k] = [one]
        return arrived

    def order(self):
        free, arrival, placed = {}, {}, []
        while len(placed) < len(self.tasks):
            best = None
            for i, (_, _, link, size, deps, hops) in enumerate(self.tasks):
                if i in arrival or any(d not in arrival for d in deps):
                    continue
                ready = max([arrival[d] for d in deps], default=0.0)
                key = (ready, i)
                if best is None or key < best[0]:
                    best = (key, i)
            (ready, _), i = best
            _, _, link, size, _, hops = self.tasks[i]
            begin = max(ready, free.get(link, 0.0))
            free[link] = begin + size / self.RATE
            arrival[i] = free[link] + self.HOP + 0.7 * (hops - 1)
            placed.append(i)
        return placed, arrival

    def run(self, copies, extra=()):
        placed, arrival = self.order()
        extra = sorted(extra, key=lambda e: e[0])
        started, waited = {}, set()

        def wait(i):
            if i not in waited:
                waited.add(i)
                started[i].wait_recv()

        for i in placed:
            ref, device, _, _, deps, _ = self.tasks[i]
            ready = max([arrival[d] for d in deps], default=0.0)
            while extra and extra[0][0] <= ready:
                extra.pop(0)[1]()
            for d in deps:
                wait(d)
            started[i] = copies.start(ref, ref, device)
        for _, call in extra:
            call()
        for i in sorted(arrival, key=arrival.get):
            wait(i)
        return [started[i] for i in placed]


def gather_plan(n_ref, t, x, c):
    core = lax.rem(t, 2)
    y, z = lax.rem(c, 4), lax.div(c, 4) * 4 + lax.div(t, 2)
    every = slice(None)
    plan = Plan()
    unit = 16 * 128 * 2

    def xx(k):
        return lax.rem(x + k + 4, 4)

    def yy(k):
        return lax.rem(y + k + 4, 4)

    def at_x(k):
        return {"row": xx(k)}

    def at_y(k):
        return {"col": lax.div(c, 4) * 4 + yy(k)}

    def at_z(k):
        zz = lax.rem(z + k + 8, 8)
        return {"tok": lax.rem(zz, 4) * 2 + core, "col": lax.div(zz, 4) * 4 + y}

    def zpos(k, first, tiles):
        zz = lax.rem(z + k + 8, 8)
        start = lax.rem(zz, 2) * QUART + first * 128
        lanes = pl.ds(pl.multiple_of(start, 128), tiles * 128)
        return lax.div(zz, 4), lax.rem(lax.div(zz, 2), 2), lanes

    rows_ab, rows_c = pl.ds(0, 3), pl.ds(3, 2)
    size_a, size_b, size_c = 6 * unit, 9 * unit, 10 * unit

    def part_a(kx, ky, kz):
        h, f, l = zpos(kz, 0, 2)
        return n_ref.at[every if kx is None else xx(kx), h, every if ky is None else yy(ky), f, rows_ab, every, l]

    def part_b(kx, ky, kz):
        h, f, l = zpos(kz, 2, 3)
        return n_ref.at[every if kx is None else xx(kx), h, every if ky is None else yy(ky), f, rows_ab, every, l]

    def part_c(kx, ky, kz):
        if kz is None:
            return n_ref.at[xx(kx), every, yy(ky), every, rows_c, every, every]
        h, f, l = zpos(kz, 0, 5)
        return n_ref.at[every if kx is None else xx(kx), h, yy(ky), f, rows_c, every, l]

    def all_of(arrived):
        return [i for ids in arrived.values() for i in ids]

    b1 = plan.straight(lambda k: part_b(0, k, 0), at_y, "y", 4, size_b, [])
    c1 = plan.straight(lambda k: part_c(0, 0, k), at_z, "z", 8, size_c, [])
    a1 = plan.straight(lambda k: part_a(k, 0, 0), at_x, "x", 4, size_a, [])
    b2 = plan.ring(lambda k: part_b(0, None, k), at_z, "z", 8, 4 * size_b, all_of(b1), 0)
    a2 = plan.straight(lambda k: part_a(None, k, 0), at_y, "y", 4, 4 * size_a, all_of(a1))
    c2 = {0: all_of(c1), 1: [], -1: [], 2: []}
    for way, k in enumerate((0, 1, -1, 2, -2, 3, -3, 4)):
        got = plan.ring(lambda kx, k=k: part_c(kx, 0, k), at_x, "x", 4, size_c, c1[k], way % 2)
        for kx in (1, -1, 2):
            c2[kx] += got[kx]
    for way, k in enumerate((0, 1, -1, 2)):
        plan.ring(lambda ky, k=k: part_c(k, ky, None), at_y, "y", 4, 8 * size_c, c2[k], way % 2)
    for way, k in enumerate((0, 1, -1, 2, -2, 3, -3, 4)):
        plan.ring(lambda kx, k=k: part_b(kx, None, k), at_x, "x", 4, 4 * size_b, b2[k], way % 2)
    for way, k in enumerate((0, 1, -1, 2)):
        plan.ring(lambda kz, k=k: part_a(None, k, kz), at_z, "z", 8, 4 * size_a, a2[k], way % 2)
    return plan


def split(v):
    high = v.astype(BF16)
    low = (v - high.astype(F32)).astype(BF16)
    return jnp.concatenate([high, low], axis=0)


def fold(v):
    return v[:COLS] + v[COLS:]


def row_of(tile):
    return jnp.concatenate([tile[k : k + 1] for k in range(4)], axis=1)


def solve_kernel(
    h_ref, g_ref, w_ref, len_ref, out_ref,
    sums, scales, halves, pieces, wt, n_ref, wbuf, d2, image, sq, other, other_sq, norm, other_norm, direction, residual,
    merged, blocks, landed, sq_send, sq_recv, send, recv,
):
    t, x, c = place()
    core, zl = lax.rem(t, 2), lax.div(t, 2)
    zh, y = lax.div(c, 4), lax.rem(c, 4)
    chip, me = x * 4 + zl, x * 8 + c
    sibling = {"tok": zl * 2 + 1 - core}

    def plane(k):
        target = lax.rem(chip + k, 16)
        return {"row": lax.div(target, 4), "tok": lax.rem(target, 4) * 2 + core}

    def block(k):
        target = lax.rem(me + k, 32)
        return {"row": lax.div(target, 8), "col": lax.rem(target, 8)}

    def line(k, side):
        return {"tok": lax.rem(zl + k, 4) * 2 + side}

    barrier = pltpu.get_barrier_semaphore()

    def greet(device):
        pl.semaphore_signal(barrier, inc=1, device_id=device, device_id_type=MESH)

    def greet_block(k, _):
        greet(block(k))
        return 0

    lax.fori_loop(1, 32, greet_block, 0)
    for k in range(1, 4):
        zz = lax.rem(zl + k, 4)
        greet(line(k, core))
        greet(line(k, 1 - core))
        greet({"tok": zz * 2 + core, "col": (1 - zh) * 4 + y})
        for kx in range(1, 4):
            greet({"row": lax.rem(x + kx, 4), "tok": zz * 2 + core})
    greet(sibling)

    h = h_ref[...].astype(F32)
    squares = jnp.sum(h * h, axis=0, keepdims=True)
    sums[me] = jnp.zeros((8, 128), F32)
    for k in range(4):
        sums[me, k : k + 1, :] = squares[:, 128 * k : 128 * k + 128]
    halves[0] = h_ref[:80]
    halves[1] = h_ref[80:]
    scales[t] = jnp.zeros((8, 128), F32)
    scales[t, 4:5, 0:80] = g_ref[:, 0:80]
    scales[t, 5:6, 0:80] = g_ref[:, 80:160]
    mine = lax.div(zl, 2)
    pieces[t] = halves[mine]
    pl.semaphore_wait(barrier, 50)

    def sums_copy(k):
        return pltpu.make_async_remote_copy(
            src_ref=sums.at[me],
            dst_ref=sums.at[me],
            send_sem=sq_send.at[k],
            recv_sem=sq_recv.at[k],
            device_id=block(k),
            device_id_type=MESH,
        )

    def send_sums(k, _):
        sums_copy(k).start()
        return 0

    def wait_sums(k, _):
        sums_copy(k).wait()
        return 0

    lax.fori_loop(1, 32, send_sums, 0)

    copies = Copies(send, recv)
    moved = []
    for k in range(1, 4):
        target = lax.rem(zl + k, 4)
        moved.append(copies.start(halves.at[lax.div(target, 2)], pieces.at[t], line(k, core)))
    handed = [copies.start(pieces.at[t], pieces.at[t], sibling)]

    eye = lax.broadcasted_iota(jnp.int32, (256, 256), 0) == lax.broadcasted_iota(jnp.int32, (256, 256), 1)
    eye = jnp.where(eye, 1.0, 0.0).astype(BF16)
    wt[...] = dot_nt(eye, w_ref[...]).astype(BF16).reshape(16, COLS, 1280)

    def w_lanes(k):
        return pl.ds(pl.multiple_of(lax.rem(lax.div(chip + 16 - k, 4), 4) * 1280, 128), 1280)

    def w_slot(k):
        return wbuf.at[lax.rem(chip + 16 - k, 4) * 2 + core, :, w_lanes(k)]

    wbuf[t, :, w_lanes(0)] = wt[chip]
    w_moved, w_handed = [], []

    def send_weights():
        for k in range(1, 16):
            w_moved.append(copies.start(wt.at[lax.rem(chip + k, 16)], w_slot(0), plane(k)))
        w_handed.append(copies.start(w_slot(0), w_slot(0), sibling))

    def hand_weights():
        for k in range(1, 16):
            w_moved[k - 1].wait_recv()
            w_handed.append(copies.start(w_slot(k), w_slot(k), sibling))

    lax.fori_loop(1, 32, wait_sums, 0)
    inverse = lax.rsqrt(jnp.sum(sums[...], axis=0) / WIDTH + EPSILON)
    slot = lax.broadcasted_iota(jnp.int32, (8, 128), 0) * 128 + lax.broadcasted_iota(jnp.int32, (8, 128), 1)
    live = (slot < len_ref[t]).astype(F32)
    scales[t, 0:4, :] = (inverse * live)[0:4]
    scaled = [copies.start(scales.at[t], scales.at[t], sibling)]
    for k in range(1, 4):
        scaled.append(copies.start(scales.at[t], scales.at[t], line(k, core)))
        scaled.append(copies.start(scales.at[t], scales.at[t], line(k, 1 - core)))
    for k in range(1, 4):
        moved[k - 1].wait_recv()
        model = lax.rem(zl + 4 - k, 4) * 2 + core
        handed.append(copies.start(pieces.at[model], pieces.at[model], sibling))
    send_weights()
    for copy in scaled + handed:
        copy.wait_recv()

    window = lax.rem(t, 4) * QUART
    source = lax.broadcasted_iota(jnp.int32, (512, QUART), 0)
    shift = source - lax.broadcasted_iota(jnp.int32, (512, QUART), 1)
    spread = lax.broadcasted_iota(jnp.int32, (80, 128), 0) == lax.broadcasted_iota(jnp.int32, (80, 128), 1)

    def add_model(m, carry):
        acc, first = carry
        size = len_ref[m]
        scale = scales[m]
        gain = jnp.where(mine == 0, scale[4:5], scale[5:6])
        gain = jnp.sum(jnp.where(spread, gain, 0.0), axis=1, keepdims=True)
        normed = (pieces[m].astype(F32) * row_of(scale) * gain).astype(BF16)
        pick = jnp.where((shift == window - first) & (source < size), 1.0, 0.0).astype(BF16)
        return acc + dot(normed, pick), first + size

    acc, _ = lax.fori_loop(0, MODELS, add_model, (jnp.zeros((80, QUART), F32), jnp.int32(0)))
    lanes = pl.ds(pl.multiple_of(lax.rem(zl, 2) * QUART, 128), QUART)
    n_ref[x, zh, y, mine, :, :, lanes] = acc.astype(BF16).reshape(5, 16, QUART)

    sent = gather_plan(n_ref, t, x, c).run(copies, [(8.0, hand_weights)])
    for copy in w_handed:
        copy.wait_recv()
    sent += moved + handed + scaled

    def block_of(xx):
        return n_ref[xx].reshape(1280, LANES)

    def features(xx):
        return slice(xx * 1280, xx * 1280 + 1280)

    def swap_image(xx, slot):
        part = features(xx)
        return copies.start(image.at[:, part], other.at[slot, :, part], sibling)

    def right_chunk(step, _):
        offset = pl.multiple_of(step * CHUNK, CHUNK)
        lane = lax.broadcasted_iota(jnp.int32, (1, CHUNK), 1) + offset
        slot = lane + core * QUART + jnp.where(lane >= QUART, QUART, 0)
        product = jnp.zeros((MODELS * COLS, CHUNK), F32)
        for xx in range(4):
            weights = wbuf[:, :, features(xx)].reshape(MODELS * COLS, 1280)
            block = n_ref[xx, :, :, :, :, :, pl.ds(offset, CHUNK)].reshape(1280, CHUNK)
            product = product + dot(weights, block)
        outputs = jnp.zeros((COLS, CHUNK), F32)
        first = jnp.int32(0)
        masks = []
        for m in range(MODELS):
            size = len_ref[m]
            mask = jnp.where((slot >= first) & (slot < first + size), 1.0, 0.0)
            first = first + size
            masks.append(mask)
            outputs = outputs + mask * product[COLS * m : COLS * m + COLS]
        masks = jnp.concatenate(masks + masks, axis=0)
        d2[:, pl.ds(offset, CHUNK)] = jnp.concatenate([outputs, masks], axis=0).astype(BF16)
        return 0

    lax.fori_loop(0, LANES // CHUNK, right_chunk, 0)
    swaps = []
    for xx in range(4):
        block = block_of(xx)
        image[:, features(xx)] = dot_nt(d2[:COLS, :LANES], block)
        swaps.append(swap_image(xx, 0))
        sq[:, features(xx)] = dot_nt(d2[COLS:, :LANES], block * block)[:MODELS]
        swaps.append(copies.start(sq.at[:, features(xx)], other_sq.at[:, features(xx)], sibling))
    for copy in swaps:
        copy.wait_recv()
    squared = sq[...] + other_sq[...]
    right = MIXING * (image[...] + other[0])
    for m in range(MODELS):
        right = right + (1.0 - MIXING) * squared[m : m + 1] * wbuf[m].astype(F32)
    diagonal = (1.0 - MIXING) * jnp.sum(squared, axis=0, keepdims=True)
    direction[...] = right
    residual[...] = right
    norm_now = jnp.sum(right * right, axis=1, keepdims=True)
    for copy in swaps:
        copy.wait_send()

    def project():
        total = jnp.zeros((2 * COLS, LANES), F32)
        for xx in range(4):
            total = total + dot(d2[:, features(xx)], block_of(xx))
        return fold(total)

    for step in range(ITERS):
        d2[...] = split(direction[...])
        if step < ITERS - 1:
            both = split(project())
            swaps = []
            for xx in range(4):
                image[:, features(xx)] = fold(dot_nt(both, block_of(xx)))
                swaps.append(swap_image(xx, step + 1))
            for copy in swaps:
                copy.wait_recv()
            now = direction[...]
            full = MIXING * (image[...] + other[step + 1]) + diagonal * now
            curvature = jnp.sum(now * full, axis=1, keepdims=True)
            step_size = norm_now / curvature
            rest = residual[...] - step_size * full
            residual[...] = rest
            norm_next = jnp.sum(rest * rest, axis=1, keepdims=True)
            if step == 0:
                merged[...] = step_size * now
            else:
                merged[...] += step_size * now
            direction[...] = rest + (norm_next / norm_now) * now
            norm_now = norm_next
            for copy in swaps:
                copy.wait_send()
        else:
            inner = project()
            inner = jnp.sum(inner * inner, axis=1, keepdims=True)
            norm[...] = jnp.broadcast_to(inner, (COLS, 128))
            swap = copies.start(norm, other_norm, sibling)
            swap.wait_recv()
            now = direction[...]
            inner = (norm[...] + other_norm[...])[:, :1]
            curvature = MIXING * inner + jnp.sum(diagonal * now * now, axis=1, keepdims=True)
            result = merged[...] + (norm_now / curvature) * now
            swap.wait_send()

    blocks[...] = jnp.zeros_like(blocks)
    for b in range(32):
        blocks[b, :, 0:160] = result[:, 160 * b : 160 * b + 160]
    landed[chip] = blocks[x * 8 + t]
    moved = []
    for k in range(1, 16):
        target = lax.rem(chip + k, 16)
        target = lax.div(target, 4) * 8 + lax.rem(target, 4) * 2 + core
        moved.append(copies.start(blocks.at[target], landed.at[chip], plane(k)))
    for copy in moved:
        copy.wait_recv()
    out_ref[...] = landed[...].reshape(256, 256)
    for copy in sent + w_moved + w_handed + moved:
        copy.wait_send()


def body(hidden, gains, weights, lengths):
    vmem = pl.BlockSpec(memory_space=pltpu.VMEM)
    wide = (COLS, WIDTH)
    count = 200
    merged = pl.pallas_call(
        solve_kernel,
        out_shape=jax.ShapeDtypeStruct((256, 256), F32),
        in_specs=[vmem, vmem, vmem, pl.BlockSpec(memory_space=pltpu.SMEM)],
        out_specs=vmem,
        scratch_shapes=[
            pltpu.VMEM((32, 8, 128), F32),
            pltpu.VMEM((MODELS, 8, 128), F32),
            pltpu.VMEM((2, 80, 512), BF16),
            pltpu.VMEM((MODELS, 80, 512), BF16),
            pltpu.VMEM((16, COLS, 1280), BF16),
            pltpu.VMEM((4, 2, 4, 2, 5, 16, LANES), BF16),
            pltpu.VMEM((MODELS, COLS, WIDTH), BF16),
            pltpu.VMEM((2 * COLS, WIDTH), BF16),
            pltpu.VMEM(wide, F32),
            pltpu.VMEM((MODELS, WIDTH), F32),
            pltpu.VMEM((ITERS, COLS, WIDTH), F32),
            pltpu.VMEM((MODELS, WIDTH), F32),
            pltpu.VMEM((COLS, 128), F32),
            pltpu.VMEM((COLS, 128), F32),
            pltpu.VMEM(wide, F32),
            pltpu.VMEM(wide, F32),
            pltpu.VMEM(wide, F32),
            pltpu.VMEM((32, COLS, 256), F32),
            pltpu.VMEM((16, COLS, 256), F32),
            pltpu.SemaphoreType.DMA((32,)),
            pltpu.SemaphoreType.DMA((32,)),
            pltpu.SemaphoreType.DMA((count,)),
            pltpu.SemaphoreType.DMA((count,)),
        ],
        compiler_params=pltpu.CompilerParams(
            collective_id=0, has_side_effects=True, vmem_limit_bytes=56 * 2**20
        ),
    )(hidden.T, gains, weights[0], lengths)
    return merged[:, :160].T


def solution(mesh):
    return jax.shard_map(
        body,
        mesh=mesh,
        in_specs=(P("tok", ("row", "col")), P("tok", ("row", "col")), P("tok", "row", "col"), P()),
        out_specs=P(("row", "tok"), "col"),
        check_vma=False,
    )
```

time: 1200 us -> 155 us (0.13)
  blocking collectives: 641 us -> 0 us
  waiting for transfers between devices: 471 us -> 0 us
  Pallas kernels: 0 us -> 153 us
  matrix products: 27.3 us -> 0 us
  local copies, waits for them, and re-layouts: 26.5 us -> 1.74 us
  other arithmetic: 17.3 us -> 0 us
  between operations: 13.3 us -> 0.01 us
    psum x9 -> x0, blocking collectives: 598 us -> none  [the longest x4 270 us: column_norms(): return lax.psum(jnp.sum(residual * residual, axis=0), ('tok', 'row'))]
    all_gather x3 -> x0, waiting for transfers between devices: 251 us -> none  [the longest x1 127 us: body(): lax.all_gather(normed, ('row', 'col'), axis=1, tiled=True)]
    reduce_scatter x6 -> x0, waiting for transfers between devices: 220 us -> none  [the longest x4 160 us: body(): lax.psum_scatter(operate_product, 'tok', scatter_dimension=0, tiled=True)]
    pallas_call x0 -> x1, Pallas kernels: none -> 153 us  [body(): pl.pallas_call(solve_kernel, out_shape=jax.ShapeDtypeStruct((256, 256), F...]
    all_gather x4 -> x0, blocking collectives: 42.9 us -> none  [body(): gathered = lax.all_gather(direction, 'row', axis=0, tiled=True)]
    dot_general x7 -> x0, matrix products: 27.3 us -> none  [the longest x4 19.4 us: body(): lax.dot_general(operator, gathered, (((0,), (0,)), ((), ())), precision=l...]
    reshape x3 -> x0, local copies, waits for them, and re-layouts: 19.5 us -> none  [the longest x2 11.8 us: body(): gram_term = gram_term.reshape(row_devices, tok_devices, sub_rows, width_dev)]
  transfers between devices with their start and end apart: 9 -> 0, of which waited for: 9 -> 0; matrix products, arithmetic and copies ran while one was open for 3% -> 0% of each run, Pallas kernels for 0% -> 0%
where the time goes in v2:
time: 155 us
  Pallas kernels  153 us (99%)
  local copies, waits for them, and re-layouts  1.74 us (1%)
    pallas_call x1, Pallas kernels, body(): pl.pallas_call(solve_kernel, out_shape=jax.ShapeDtypeStruct((256, 256), F...  153 us

profile of v2, /device:TPU:1, one launch (start us, length us, event | category | flops | bytes accessed | tf_op | source)
XLA Modules:
  0.0 154.7 jit_solution(602352832487927495)
XLA Ops:
  0.0 152.9 %shard_map.46 = f32[256,256]{1,0:T(8,128)} custom-call(bf16[160,512]{1,0:T(8,128)(2,1)} %bitcast.5, f32[1,160]{1,0:T(1,128)} %g_ref.1, bf16[1280,256]{1,0:T(8,128)(2,1)} %bitcast.4, s32[8]{0:T(128)} %len_ref.1), custom_call_target="tpu_custom_call" | custom-call | tf_op jit(solution)/shard_map/pallas_call | solution.py:481
  153.0 1.0 slice_bitcast_fusion
  153.9 0.8 copy.5

commit v3 on v2

--- a/solution.py
+++ b/solution.py
@@ -16,6 +16,7 @@
 MODELS = 8
 QUART = 640
 LANES = 2 * QUART
+LIVE = 2304
 CHUNK = 256
 COLS = 16
 
@@ -91,26 +92,29 @@
         return arrived
 
     def order(self):
-        free, arrival, placed = {}, {}, []
-        while len(placed) < len(self.tasks):
-            best = None
-            for i, (_, _, link, size, deps, hops) in enumerate(self.tasks):
-                if i in arrival or any(d not in arrival for d in deps):
-                    continue
-                ready = max([arrival[d] for d in deps], default=0.0)
-                key = (ready, i)
-                if best is None or key < best[0]:
-                    best = (key, i)
-            (ready, _), i = best
-            _, _, link, size, _, hops = self.tasks[i]
-            begin = max(ready, free.get(link, 0.0))
-            free[link] = begin + size / self.RATE
-            arrival[i] = free[link] + self.HOP + 0.7 * (hops - 1)
-            placed.append(i)
-        return placed, arrival
+        count = len(self.tasks)
+        rank = [0.0] * count
+        for i in reversed(range(count)):
+            _, _, _, size, deps, hops = self.tasks[i]
+            rank[i] += size / self.RATE + self.HOP + 0.7 * (hops - 1)
+            for d in deps:
+                rank[d] = max(rank[d], rank[i])
+        free, arrival, placed, begins = {}, {}, [], {}
+        while len(placed) < count:
+            ready = {}
+            for i, (_, _, link, _, deps, _) in enumerate(self.tasks):
+                if i not in arrival and all(d in arrival for d in deps):
+                    ready[i] = max([arrival[d] for d in deps] + [free.get(link, 0.0)])
+            first = min(ready, key=lambda i: (round(ready[i], 3), -rank[i], i))
+            _, _, link, size, _, hops = self.tasks[first]
+            begins[first] = ready[first]
+            free[link] = ready[first] + size / self.RATE
+            arrival[first] = free[link] + self.HOP + 0.7 * (hops - 1)
+            placed.append(first)
+        return placed, arrival, begins
 
     def run(self, copies, extra=()):
-        placed, arrival = self.order()
+        placed, arrival, begins = self.order()
         extra = sorted(extra, key=lambda e: e[0])
         started, waited = {}, set()
 
@@ -121,8 +125,7 @@
 
         for i in placed:
             ref, device, _, _, deps, _ = self.tasks[i]
-            ready = max([arrival[d] for d in deps], default=0.0)
-            while extra and extra[0][0] <= ready:
+            while extra and extra[0][0] <= begins[i]:
                 extra.pop(0)[1]()
             for d in deps:
                 wait(d)
@@ -184,17 +187,20 @@
         return [i for ids in arrived.values() for i in ids]
 
     b1 = plan.straight(lambda k: part_b(0, k, 0), at_y, "y", 4, size_b, [])
-    c1 = plan.straight(lambda k: part_c(0, 0, k), at_z, "z", 8, size_c, [])
+    c1 = plan.ring(lambda k: part_c(0, 0, k), at_z, "z", 8, size_c, [], 1)
     a1 = plan.straight(lambda k: part_a(k, 0, 0), at_x, "x", 4, size_a, [])
     b2 = plan.ring(lambda k: part_b(0, None, k), at_z, "z", 8, 4 * size_b, all_of(b1), 0)
-    a2 = plan.straight(lambda k: part_a(None, k, 0), at_y, "y", 4, 4 * size_a, all_of(a1))
+    a2 = plan.ring(lambda k: part_a(None, k, 0), at_y, "y", 4, 4 * size_a, all_of(a1), 1)
     c2 = {0: all_of(c1), 1: [], -1: [], 2: []}
+    c2z = {}
     for way, k in enumerate((0, 1, -1, 2, -2, 3, -3, 4)):
         got = plan.ring(lambda kx, k=k: part_c(kx, 0, k), at_x, "x", 4, size_c, c1[k], way % 2)
         for kx in (1, -1, 2):
             c2[kx] += got[kx]
+        c2z[k] = got
     for way, k in enumerate((0, 1, -1, 2)):
-        plan.ring(lambda ky, k=k: part_c(k, ky, None), at_y, "y", 4, 8 * size_c, c2[k], way % 2)
+        for kz in (0, 1, -1, 2, -2, 3, -3, 4):
+            plan.ring(lambda ky, k=k, kz=kz: part_c(k, ky, kz), at_y, "y", 4, size_c, c2z[kz][k], (way + kz) % 2)
     for way, k in enumerate((0, 1, -1, 2, -2, 3, -3, 4)):
         plan.ring(lambda kx, k=k: part_b(kx, None, k), at_x, "x", 4, 4 * size_b, b2[k], way % 2)
     for way, k in enumerate((0, 1, -1, 2)):
@@ -219,7 +225,8 @@
 def solve_kernel(
     h_ref, g_ref, w_ref, len_ref, out_ref,
     sums, scales, halves, pieces, wt, n_ref, wbuf, d2, image, sq, other, other_sq, norm, other_norm, direction, residual,
-    merged, blocks, landed, sq_send, sq_recv, send, recv,
+    merged, diagonal, squared_norm, size, ub, blocks, landed, last_blocks, last_landed, sq_send, sq_recv,
+    swap_send, swap_recv, norm_send, norm_recv, out_send, out_recv, send, recv,
 ):
     t, x, c = place()
     core, zl = lax.rem(t, 2), lax.div(t, 2)
@@ -269,6 +276,8 @@
     scales[t, 5:6, 0:80] = g_ref[:, 80:160]
     mine = lax.div(zl, 2)
     pieces[t] = halves[mine]
+    blocks[...] = jnp.zeros_like(blocks)
+    last_blocks[...] = jnp.zeros_like(last_blocks)
     pl.semaphore_wait(barrier, 50)
 
     def sums_copy(k):
@@ -339,21 +348,32 @@
         copy.wait_recv()
 
     window = lax.rem(t, 4) * QUART
-    source = lax.broadcasted_iota(jnp.int32, (512, QUART), 0)
-    shift = source - lax.broadcasted_iota(jnp.int32, (512, QUART), 1)
+    shift = lax.broadcasted_iota(jnp.int32, (512, QUART), 0)
+    shift = shift - lax.broadcasted_iota(jnp.int32, (512, QUART), 1)
     spread = lax.broadcasted_iota(jnp.int32, (80, 128), 0) == lax.broadcasted_iota(jnp.int32, (80, 128), 1)
 
+    lane = lax.broadcasted_iota(jnp.int32, (80, 128), 1)
+
     def add_model(m, carry):
-        acc, first = carry
+        acc, tile, first = carry
         size = len_ref[m]
         scale = scales[m]
         gain = jnp.where(mine == 0, scale[4:5], scale[5:6])
         gain = jnp.sum(jnp.where(spread, gain, 0.0), axis=1, keepdims=True)
         normed = (pieces[m].astype(F32) * row_of(scale) * gain).astype(BF16)
-        pick = jnp.where((shift == window - first) & (source < size), 1.0, 0.0).astype(BF16)
-        return acc + dot(normed, pick), first + size
-
-    acc, _ = lax.fori_loop(0, MODELS, add_model, (jnp.zeros((80, QUART), F32), jnp.int32(0)))
+        pick = jnp.where(shift == window - first, 1.0, 0.0).astype(BF16)
+        wide_normed = normed.astype(F32)
+        total = jnp.sum(wide_normed * wide_normed, axis=1, keepdims=True)
+        tile = jnp.where(lax.rem(lane, 8) == m, total, tile)
+        return acc + dot(normed, pick), tile, first + size
+
+    zero = (jnp.zeros((80, QUART), F32), jnp.zeros((80, 128), F32), jnp.int32(0))
+    acc, tile, _ = lax.fori_loop(0, MODELS, add_model, zero)
+    high = tile.astype(BF16).astype(F32)
+    middle = (tile - high).astype(BF16).astype(F32)
+    tile = jnp.where(lane < 8, high, jnp.where(lane < 16, middle, tile - high - middle))
+    tile = jnp.where(lane < 24, tile, 0.0)
+    acc = jnp.concatenate([acc[:, :512], acc[:, 512:] + jnp.where(lax.rem(t, 4) == 3, tile, 0.0)], axis=1)
     lanes = pl.ds(pl.multiple_of(lax.rem(zl, 2) * QUART, 128), QUART)
     n_ref[x, zh, y, mine, :, :, lanes] = acc.astype(BF16).reshape(5, 16, QUART)
 
@@ -366,121 +386,215 @@
         return n_ref[xx].reshape(1280, LANES)
 
     def features(xx):
-        return slice(xx * 1280, xx * 1280 + 1280)
-
-    def swap_image(xx, slot):
-        part = features(xx)
-        return copies.start(image.at[:, part], other.at[slot, :, part], sibling)
+        return pl.ds(pl.multiple_of(xx * 1280, 128), 1280)
+
+    def each(body, init=0):
+        return lax.fori_loop(0, 4, body, init)
+
+    def fold_lanes(v):
+        return functools.reduce(jnp.add, [v[:, 128 * k : 128 * k + 128] for k in range(10)])
+
+    def swap_copy(slot, xx):
+        return pltpu.make_async_remote_copy(
+            src_ref=image.at[:, features(xx)],
+            dst_ref=other.at[slot, :, features(xx)],
+            send_sem=swap_send.at[slot * 4 + xx],
+            recv_sem=swap_recv.at[slot * 4 + xx],
+            device_id=sibling,
+            device_id_type=MESH,
+        )
+
+    def norm_copy(step):
+        return pltpu.make_async_remote_copy(
+            src_ref=norm.at[step],
+            dst_ref=other_norm.at[step],
+            send_sem=norm_send.at[step],
+            recv_sem=norm_recv.at[step],
+            device_id=sibling,
+            device_id_type=MESH,
+        )
+
+    def slots(first, count):
+        at = lax.broadcasted_iota(jnp.int32, (1, count), 1) + first
+        return at + core * QUART + jnp.where(at >= QUART, QUART, 0)
+
+    take = lax.broadcasted_iota(jnp.int32, (16, 128), 1)
+    take = (lax.rem(take, 8) == lax.broadcasted_iota(jnp.int32, (16, 128), 0)) & (take < 24)
+    take = jnp.where(take, 1.0, 0.0).astype(BF16)
+
+    def squares_part(xx, _):
+        spare = n_ref[xx, :, :, :, :, :, LANES - 128 :].reshape(1280, 128)
+        sq[:, features(xx)] = dot_nt(take, spare)[:MODELS]
+        return 0
+
+    each(squares_part)
+    swap_sq = copies.start(sq, other_sq, sibling)
 
     def right_chunk(step, _):
         offset = pl.multiple_of(step * CHUNK, CHUNK)
-        lane = lax.broadcasted_iota(jnp.int32, (1, CHUNK), 1) + offset
-        slot = lane + core * QUART + jnp.where(lane >= QUART, QUART, 0)
+        slot = slots(offset, CHUNK)
         product = jnp.zeros((MODELS * COLS, CHUNK), F32)
         for xx in range(4):
-            weights = wbuf[:, :, features(xx)].reshape(MODELS * COLS, 1280)
+            weights = wbuf[:, :, xx * 1280 : xx * 1280 + 1280].reshape(MODELS * COLS, 1280)
             block = n_ref[xx, :, :, :, :, :, pl.ds(offset, CHUNK)].reshape(1280, CHUNK)
             product = product + dot(weights, block)
         outputs = jnp.zeros((COLS, CHUNK), F32)
         first = jnp.int32(0)
-        masks = []
         for m in range(MODELS):
             size = len_ref[m]
             mask = jnp.where((slot >= first) & (slot < first + size), 1.0, 0.0)
             first = first + size
-            masks.append(mask)
             outputs = outputs + mask * product[COLS * m : COLS * m + COLS]
-        masks = jnp.concatenate(masks + masks, axis=0)
-        d2[:, pl.ds(offset, CHUNK)] = jnp.concatenate([outputs, masks], axis=0).astype(BF16)
+        ub[:COLS, pl.ds(offset, CHUNK)] = outputs.astype(BF16)
         return 0
 
-    lax.fori_loop(0, LANES // CHUNK, right_chunk, 0)
-    swaps = []
-    for xx in range(4):
-        block = block_of(xx)
-        image[:, features(xx)] = dot_nt(d2[:COLS, :LANES], block)
-        swaps.append(swap_image(xx, 0))
-        sq[:, features(xx)] = dot_nt(d2[COLS:, :LANES], block * block)[:MODELS]
-        swaps.append(copies.start(sq.at[:, features(xx)], other_sq.at[:, features(xx)], sibling))
-    for copy in swaps:
-        copy.wait_recv()
-    squared = sq[...] + other_sq[...]
-    right = MIXING * (image[...] + other[0])
-    for m in range(MODELS):
-        right = right + (1.0 - MIXING) * squared[m : m + 1] * wbuf[m].astype(F32)
-    diagonal = (1.0 - MIXING) * jnp.sum(squared, axis=0, keepdims=True)
-    direction[...] = right
-    residual[...] = right
-    norm_now = jnp.sum(right * right, axis=1, keepdims=True)
-    for copy in swaps:
-        copy.wait_send()
-
-    def project():
-        total = jnp.zeros((2 * COLS, LANES), F32)
-        for xx in range(4):
-            total = total + dot(d2[:, features(xx)], block_of(xx))
-        return fold(total)
-
-    for step in range(ITERS):
-        d2[...] = split(direction[...])
-        if step < ITERS - 1:
-            both = split(project())
-            swaps = []
+    def right_part(xx, total):
+        swap_copy(0, xx).wait_recv()
+        part = features(xx)
+        right = MIXING * (image[:, part] + other[0, :, part])
+        squared = jnp.where(core == 1, sq[:, part], other_sq[:, part])
+        for m in range(MODELS):
+            right = right + (1.0 - MIXING) * squared[m : m + 1] * wbuf[m, :, part].astype(F32)
+        diagonal[0:1, part] = (1.0 - MIXING) * jnp.sum(squared, axis=0, keepdims=True)
+        direction[:, part] = right
+        residual[:, part] = right
+        d2[:, part] = split(right)
+        return total + fold_lanes(right * right)
+
+    def spread_out(v):
+        return jnp.broadcast_to(jnp.sum(v, axis=1, keepdims=True), (COLS, 128))
+
+    def block_copy(k, source, target, first):
+        to = lax.rem(chip + k, 16)
+        to = lax.div(to, 4) * 8 + lax.rem(to, 4) * 2 + core
+        return pltpu.make_async_remote_copy(
+            src_ref=source.at[to],
+            dst_ref=target.at[chip],
+            send_sem=out_send.at[first + k],
+            recv_sem=out_recv.at[first + k],
+            device_id=plane(k),
+            device_id_type=MESH,
+        )
+
+    def send_blocks(values, source, target, first):
+        def cut(group, _):
+            value = values(pl.ds(pl.multiple_of(group * 640, 128), 640))
+            for k in range(4):
+                source[group * 4 + k, :, 0:160] = value[:, 160 * k : 160 * k + 160].astype(source.dtype)
+            return 0
+
+        def send_one(k, _):
+            block_copy(k, source, target, first).start()
+            return 0
+
+        lax.fori_loop(0, 8, cut, 0)
+        target[chip] = source[x * 8 + t]
+        lax.fori_loop(1, 16, send_one, 0)
+
+    def solve_step(step, _):
+        @pl.when(step == 0)
+        def _():
+            lax.fori_loop(0, LANES // CHUNK, right_chunk, 0)
+            ub[COLS:] = jnp.zeros((COLS, LANES), BF16)
+
+        @pl.when(step > 0)
+        def _():
+            total = jnp.zeros((2 * COLS, LANES), F32)
             for xx in range(4):
-                image[:, features(xx)] = fold(dot_nt(both, block_of(xx)))
-                swaps.append(swap_image(xx, step + 1))
-            for copy in swaps:
-                copy.wait_recv()
-            now = direction[...]
-            full = MIXING * (image[...] + other[step + 1]) + diagonal * now
-            curvature = jnp.sum(now * full, axis=1, keepdims=True)
-            step_size = norm_now / curvature
-            rest = residual[...] - step_size * full
-            residual[...] = rest
-            norm_next = jnp.sum(rest * rest, axis=1, keepdims=True)
-            if step == 0:
-                merged[...] = step_size * now
-            else:
-                merged[...] += step_size * now
-            direction[...] = rest + (norm_next / norm_now) * now
-            norm_now = norm_next
-            for copy in swaps:
-                copy.wait_send()
-        else:
-            inner = project()
-            inner = jnp.sum(inner * inner, axis=1, keepdims=True)
-            norm[...] = jnp.broadcast_to(inner, (COLS, 128))
-            swap = copies.start(norm, other_norm, sibling)
-            swap.wait_recv()
-            now = direction[...]
-            inner = (norm[...] + other_norm[...])[:, :1]
-            curvature = MIXING * inner + jnp.sum(diagonal * now * now, axis=1, keepdims=True)
-            result = merged[...] + (norm_now / curvature) * now
-            swap.wait_send()
-
-    blocks[...] = jnp.zeros_like(blocks)
-    for b in range(32):
-        blocks[b, :, 0:160] = result[:, 160 * b : 160 * b + 160]
-    landed[chip] = blocks[x * 8 + t]
-    moved = []
-    for k in range(1, 16):
-        target = lax.rem(chip + k, 16)
-        target = lax.div(target, 4) * 8 + lax.rem(target, 4) * 2 + core
-        moved.append(copies.start(blocks.at[target], landed.at[chip], plane(k)))
-    for copy in moved:
-        copy.wait_recv()
-    out_ref[...] = landed[...].reshape(256, 256)
-    for copy in sent + w_moved + w_handed + moved:
+                total = total + dot(d2[:, 1280 * xx : 1280 * xx + 1280], block_of(xx))
+            projected = fold(total) * jnp.where(slots(0, LANES) < LIVE, 1.0, 0.0)
+            norm[step] = spread_out(fold_lanes(projected * projected))
+            norm_copy(step).start()
+            ub[...] = split(projected)
+
+        @pl.when(step < ITERS)
+        def _():
+            def back_part(xx, _):
+                image[:, features(xx)] = fold(dot_nt(ub[...], block_of(xx)))
+                swap_copy(step, xx).start()
+                return 0
+
+            each(back_part)
+
+        @pl.when(step == 0)
+        def _():
+            swap_sq.wait()
+            squared_norm[...] = spread_out(each(right_part, jnp.zeros((COLS, 128), F32)))
+            merged[...] = jnp.zeros_like(merged)
+
+        @pl.when(step > 0)
+        def _():
+            def weighted(xx, total):
+                now = direction[:, features(xx)]
+                return total + fold_lanes(diagonal[0:1, features(xx)] * now * now)
+
+            inner = spread_out(each(weighted, jnp.zeros((COLS, 128), F32)))
+            norm_copy(step).wait()
+            curvature = MIXING * (norm[step] + other_norm[step]) + inner
+            size[...] = squared_norm[...] / curvature
+
+        @pl.when((step > 0) & (step < ITERS))
+        def _():
+            factor = size[:, :1]
+            merged[...] += factor * direction[...]
+
+            @pl.when(step == ITERS - 1)
+            def _():
+                send_blocks(lambda part: merged[:, part], blocks, landed, 0)
+
+            def residual_part(xx, total):
+                part = features(xx)
+                swap_copy(step, xx).wait_recv()
+                full = MIXING * (image[:, part] + other[step, :, part]) + diagonal[0:1, part] * direction[:, part]
+                rest = residual[:, part] - factor * full
+                residual[:, part] = rest
+                return total + fold_lanes(rest * rest)
+
+            norm_next = spread_out(each(residual_part, jnp.zeros((COLS, 128), F32)))
+            ratio = (norm_next / squared_norm[...])[:, :1]
+            squared_norm[...] = norm_next
+
+            def direction_part(xx, _):
+                part = features(xx)
+                now = residual[:, part] + ratio * direction[:, part]
+                direction[:, part] = now
+                d2[:, part] = split(now)
+                return 0
+
+            each(direction_part)
+
+        @pl.when(step < ITERS)
+        def _():
+            def sent_part(xx, _):
+                swap_copy(step, xx).wait_send()
+                return 0
+
+            each(sent_part)
+
+        return 0
+
+    lax.fori_loop(0, ITERS + 1, solve_step, 0)
+    send_blocks(lambda part: size[:, :1] * direction[:, part], last_blocks, last_landed, 16)
+
+    def wait_blocks(k, _):
+        block_copy(k, blocks, landed, 0).wait()
+        block_copy(k, last_blocks, last_landed, 16).wait()
+        return 0
+
+    lax.fori_loop(1, 16, wait_blocks, 0)
+    result = landed[...] + last_landed[...].astype(F32)
+    out_ref[...] = result.reshape(256, 256).T[:160]
+    for copy in sent + w_moved + w_handed:
         copy.wait_send()
 
 
 def body(hidden, gains, weights, lengths):
     vmem = pl.BlockSpec(memory_space=pltpu.VMEM)
     wide = (COLS, WIDTH)
-    count = 200
-    merged = pl.pallas_call(
+    count = 250
+    return pl.pallas_call(
         solve_kernel,
-        out_shape=jax.ShapeDtypeStruct((256, 256), F32),
+        out_shape=jax.ShapeDtypeStruct((160, 256), F32),
         in_specs=[vmem, vmem, vmem, pl.BlockSpec(memory_space=pltpu.SMEM)],
         out_specs=vmem,
         scratch_shapes=[
@@ -496,13 +610,25 @@
             pltpu.VMEM((MODELS, WIDTH), F32),
             pltpu.VMEM((ITERS, COLS, WIDTH), F32),
             pltpu.VMEM((MODELS, WIDTH), F32),
-            pltpu.VMEM((COLS, 128), F32),
-            pltpu.VMEM((COLS, 128), F32),
+            pltpu.VMEM((ITERS + 1, COLS, 128), F32),
+            pltpu.VMEM((ITERS + 1, COLS, 128), F32),
             pltpu.VMEM(wide, F32),
             pltpu.VMEM(wide, F32),
             pltpu.VMEM(wide, F32),
+            pltpu.VMEM((8, WIDTH), F32),
+            pltpu.VMEM((COLS, 128), F32),
+            pltpu.VMEM((COLS, 128), F32),
+            pltpu.VMEM((2 * COLS, LANES), BF16),
             pltpu.VMEM((32, COLS, 256), F32),
             pltpu.VMEM((16, COLS, 256), F32),
+            pltpu.VMEM((32, COLS, 256), BF16),
+            pltpu.VMEM((16, COLS, 256), BF16),
+            pltpu.SemaphoreType.DMA((32,)),
+            pltpu.SemaphoreType.DMA((32,)),
+            pltpu.SemaphoreType.DMA((4 * ITERS,)),
+            pltpu.SemaphoreType.DMA((4 * ITERS,)),
+            pltpu.SemaphoreType.DMA((ITERS + 1,)),
+            pltpu.SemaphoreType.DMA((ITERS + 1,)),
             pltpu.SemaphoreType.DMA((32,)),
             pltpu.SemaphoreType.DMA((32,)),
             pltpu.SemaphoreType.DMA((count,)),
@@ -512,7 +638,6 @@
             collective_id=0, has_side_effects=True, vmem_limit_bytes=56 * 2**20
         ),
     )(hidden.T, gains, weights[0], lengths)
-    return merged[:, :160].T
 
 
 def solution(mesh):

time: 155 us -> 145 us (0.935)
  Pallas kernels: 153 us -> 143 us
    pallas_call x1, Pallas kernels: 153 us -> 143 us  [body(): pl.pallas_call(solve_kernel, out_shape=jax.ShapeDtypeStruct((160, 256), F...]
    transpose x2 -> x0, local copies, waits for them, and re-layouts: 1.74 us -> none  [body(): return merged[:, :160].T]
    unnamed x0 -> x1, local copies, waits for them, and re-layouts: none -> 1.59 us
where the time goes in v3:
time: 145 us
  Pallas kernels  143 us (99%)
  local copies, waits for them, and re-layouts  1.59 us (1%)
    pallas_call x1, Pallas kernels, body(): pl.pallas_call(solve_kernel, out_shape=jax.ShapeDtypeStruct((160, 256), F...  143 us

profile of v3, /device:TPU:1, one launch (start us, length us, event | category | flops | bytes accessed | tf_op | source)
XLA Modules:
  0.0 144.7 jit_solution(14787341929497226512)
XLA Ops:
  0.0 143.1 %shard_map.46 = f32[160,256]{1,0:T(8,128)} custom-call(bf16[160,512]{1,0:T(8,128)(2,1)} %bitcast.3, f32[1,160]{1,0:T(1,128)} %g_ref.1, bf16[1280,256]{1,0:T(8,128)(2,1)} %bitcast.2, s32[8]{0:T(128)} %len_ref.1), custom_call_target="tpu_custom_call" | custom-call | tf_op jit(solution)/shard_map/pallas_call | solution.py:595
  143.1 1.6 %copy.6 = f32[160,256]{1,0:T(8,128)} copy(f32[160,256]{1,0:T(8,128)} %shard_map.46) | data formatting | bytes 327680

commit v4 on v3

--- a/solution.py
+++ b/solution.py
@@ -58,24 +58,25 @@
     RATE, HOP = 45e3, 2.3
 
     def __init__(self):
-        self.tasks = []
-
-    def add(self, ref, device, link, size, deps, hops=1):
+        self.tasks, self.level = [], []
+
+    def add(self, ref, device, link, size, deps, hops=1, level=0):
         self.tasks.append((ref, device, link, size, tuple(deps), hops))
+        self.level.append(level)
         return len(self.tasks) - 1
 
-    def ring(self, ref, device, axis, n, size, deps, way):
-        deps = list(deps)
-        right = [self.add(ref(0), device(1), axis + "+", size, deps)]
-        left = [self.add(ref(0), device(-1), axis + "-", size, deps)]
+    def ring(self, ref, device, axis, n, size, deps, way, level=0, far_level=None):
+        deps, far_level = list(deps), level if far_level is None else far_level
+        right = [self.add(ref(0), device(1), axis + "+", size, deps, 1, level)]
+        left = [self.add(ref(0), device(-1), axis + "-", size, deps, 1, level)]
         for k in range(1, n // 2 - 1):
-            right.append(self.add(ref(-k), device(1), axis + "+", size, right[-1:]))
-            left.append(self.add(ref(k), device(-1), axis + "-", size, left[-1:]))
+            right.append(self.add(ref(-k), device(1), axis + "+", size, right[-1:], 1, level))
+            left.append(self.add(ref(k), device(-1), axis + "-", size, left[-1:], 1, level))
         last = n // 2 - 1
         if way == 0:
-            far = self.add(ref(-last), device(1), axis + "+", size, right[-1:])
+            far = self.add(ref(-last), device(1), axis + "+", size, right[-1:], 1, far_level)
         else:
-            far = self.add(ref(last), device(-1), axis + "-", size, left[-1:])
+            far = self.add(ref(last), device(-1), axis + "-", size, left[-1:], 1, far_level)
         arrived = {0: deps, n // 2: [far]}
         for k in range(1, n // 2):
             arrived[-k] = [right[k - 1]]
@@ -105,7 +106,7 @@
             for i, (_, _, link, _, deps, _) in enumerate(self.tasks):
                 if i not in arrival and all(d in arrival for d in deps):
                     ready[i] = max([arrival[d] for d in deps] + [free.get(link, 0.0)])
-            first = min(ready, key=lambda i: (round(ready[i], 3), -rank[i], i))
+            first = min(ready, key=lambda i: (round(ready[i], 3), self.level[i], -rank[i], i))
             _, _, link, size, _, hops = self.tasks[first]
             begins[first] = ready[first]
             free[link] = ready[first] + size / self.RATE
@@ -113,27 +114,31 @@
             placed.append(first)
         return placed, arrival, begins
 
-    def run(self, copies, extra=()):
+    def run(self, copies, extra):
         placed, arrival, begins = self.order()
+        extra = [(max([at] + [arrival[d] for d in deps]), deps, call) for at, deps, call in extra]
         extra = sorted(extra, key=lambda e: e[0])
         started, waited = {}, set()
 
-        def wait(i):
-            if i not in waited:
-                waited.add(i)
-                started[i].wait_recv()
+        def wait(ids):
+            for i in sorted(ids, key=arrival.get):
+                if i not in waited:
+                    waited.add(i)
+                    started[i].wait_recv()
+
+        def due(now):
+            while extra and extra[0][0] + 0.5 <= now:
+                _, deps, call = extra.pop(0)
+                wait(deps)
+                call()
 
         for i in placed:
             ref, device, _, _, deps, _ = self.tasks[i]
-            while extra and extra[0][0] <= begins[i]:
-                extra.pop(0)[1]()
-            for d in deps:
-                wait(d)
+            due(begins[i])
+            wait(deps)
             started[i] = copies.start(ref, ref, device)
-        for _, call in extra:
-            call()
-        for i in sorted(arrival, key=arrival.get):
-            wait(i)
+        due(1e9)
+        wait(arrival)
         return [started[i] for i in placed]
 
 
@@ -191,21 +196,29 @@
     a1 = plan.straight(lambda k: part_a(k, 0, 0), at_x, "x", 4, size_a, [])
     b2 = plan.ring(lambda k: part_b(0, None, k), at_z, "z", 8, 4 * size_b, all_of(b1), 0)
     a2 = plan.ring(lambda k: part_a(None, k, 0), at_y, "y", 4, 4 * size_a, all_of(a1), 1)
-    c2 = {0: all_of(c1), 1: [], -1: [], 2: []}
-    c2z = {}
+    turns = ((0, 0), (1, 1), (-1, 1), (2, 2))
+    whole = {0: all_of(b2), 1: [], -1: [], 2: []}
+    c2 = {}
     for way, k in enumerate((0, 1, -1, 2, -2, 3, -3, 4)):
-        got = plan.ring(lambda kx, k=k: part_c(kx, 0, k), at_x, "x", 4, size_c, c1[k], way % 2)
+        c2[k] = plan.ring(lambda kx, k=k: part_c(kx, 0, k), at_x, "x", 4, size_c, c1[k], way % 2)
+    for way, (k, level) in enumerate(turns):
+        for kz in (0, 1, -1, 2, -2, 3, -3, 4):
+            got = plan.ring(
+                lambda ky, k=k, kz=kz: part_c(k, ky, kz), at_y, "y", 4, size_c, c2[kz][k], way % 2, level
+            )
+            whole[k] += all_of(got)
+    for way, k in enumerate((0, 1, -1, 2, -2, 3, -3, 4)):
+        got = plan.ring(
+            lambda kx, k=k: part_b(kx, None, k), at_x, "x", 4, 4 * size_b, b2[k], way % 2, 1, 2
+        )
         for kx in (1, -1, 2):
-            c2[kx] += got[kx]
-        c2z[k] = got
-    for way, k in enumerate((0, 1, -1, 2)):
-        for kz in (0, 1, -1, 2, -2, 3, -3, 4):
-            plan.ring(lambda ky, k=k, kz=kz: part_c(k, ky, kz), at_y, "y", 4, size_c, c2z[kz][k], (way + kz) % 2)
-    for way, k in enumerate((0, 1, -1, 2, -2, 3, -3, 4)):
-        plan.ring(lambda kx, k=k: part_b(kx, None, k), at_x, "x", 4, 4 * size_b, b2[k], way % 2)
-    for way, k in enumerate((0, 1, -1, 2)):
-        plan.ring(lambda kz, k=k: part_a(None, k, kz), at_z, "z", 8, 4 * size_a, a2[k], way % 2)
-    return plan
+            whole[kx] += got[kx]
+    for way, (k, level) in enumerate(turns):
+        got = plan.ring(
+            lambda kz, k=k: part_a(k, None, kz), at_z, "z", 8, 4 * size_a, all_of(a2), way % 2, level
+        )
+        whole[k] += all_of(got)
+    return plan, whole
 
 
 def split(v):
@@ -225,7 +238,7 @@
 def solve_kernel(
     h_ref, g_ref, w_ref, len_ref, out_ref,
     sums, scales, halves, pieces, wt, n_ref, wbuf, d2, image, sq, other, other_sq, norm, other_norm, direction, residual,
-    merged, diagonal, squared_norm, size, ub, blocks, landed, last_blocks, last_landed, sq_send, sq_recv,
+    merged, diagonal, squared_norm, size, ub, product, turned, blocks, landed, last_blocks, last_landed, sq_send, sq_recv,
     swap_send, swap_recv, norm_send, norm_recv, out_send, out_recv, send, recv,
 ):
     t, x, c = place()
@@ -377,11 +390,6 @@
     lanes = pl.ds(pl.multiple_of(lax.rem(zl, 2) * QUART, 128), QUART)
     n_ref[x, zh, y, mine, :, :, lanes] = acc.astype(BF16).reshape(5, 16, QUART)
 
-    sent = gather_plan(n_ref, t, x, c).run(copies, [(8.0, hand_weights)])
-    for copy in w_handed:
-        copy.wait_recv()
-    sent += moved + handed + scaled
-
     def block_of(xx):
         return n_ref[xx].reshape(1280, LANES)
 
@@ -422,31 +430,31 @@
     take = (lax.rem(take, 8) == lax.broadcasted_iota(jnp.int32, (16, 128), 0)) & (take < 24)
     take = jnp.where(take, 1.0, 0.0).astype(BF16)
 
-    def squares_part(xx, _):
+    def use_block(k):
+        xx = lax.rem(x + k + 4, 4)
         spare = n_ref[xx, :, :, :, :, :, LANES - 128 :].reshape(1280, 128)
         sq[:, features(xx)] = dot_nt(take, spare)[:MODELS]
-        return 0
-
-    each(squares_part)
+        weights = wbuf[:, :, features(xx)].reshape(MODELS * COLS, 1280)
+
+        def part(step, _):
+            at = pl.ds(pl.multiple_of(step * CHUNK, CHUNK), CHUNK)
+            block = n_ref[xx, :, :, :, :, :, at].reshape(1280, CHUNK)
+            turned[xx, at, :] = block.T
+            more = dot(weights, block)
+            product[:, at] = more if k == 0 else product[:, at] + more
+            return 0
+
+        lax.fori_loop(0, LANES // CHUNK, part, 0)
+
+    def wait_weights():
+        for copy in w_handed:
+            copy.wait_recv()
+
+    plan, whole = gather_plan(n_ref, t, x, c)
+    first = [(8.0, [], hand_weights), (0.0, whole[0], wait_weights)]
+    sent = plan.run(copies, first + [(0.0, whole[k], functools.partial(use_block, k)) for k in (0, 1, -1, 2)])
+    sent += moved + handed + scaled
     swap_sq = copies.start(sq, other_sq, sibling)
-
-    def right_chunk(step, _):
-        offset = pl.multiple_of(step * CHUNK, CHUNK)
-        slot = slots(offset, CHUNK)
-        product = jnp.zeros((MODELS * COLS, CHUNK), F32)
-        for xx in range(4):
-            weights = wbuf[:, :, xx * 1280 : xx * 1280 + 1280].reshape(MODELS * COLS, 1280)
-            block = n_ref[xx, :, :, :, :, :, pl.ds(offset, CHUNK)].reshape(1280, CHUNK)
-            product = product + dot(weights, block)
-        outputs = jnp.zeros((COLS, CHUNK), F32)
-        first = jnp.int32(0)
-        for m in range(MODELS):
-            size = len_ref[m]
-            mask = jnp.where((slot >= first) & (slot < first + size), 1.0, 0.0)
-            first = first + size
-            outputs = outputs + mask * product[COLS * m : COLS * m + COLS]
-        ub[:COLS, pl.ds(offset, CHUNK)] = outputs.astype(BF16)
-        return 0
 
     def right_part(xx, total):
         swap_copy(0, xx).wait_recv()
@@ -494,7 +502,15 @@
     def solve_step(step, _):
         @pl.when(step == 0)
         def _():
-            lax.fori_loop(0, LANES // CHUNK, right_chunk, 0)
+            slot = slots(0, LANES)
+            outputs = jnp.zeros((COLS, LANES), F32)
+            first = jnp.int32(0)
+            for m in range(MODELS):
+                size = len_ref[m]
+                mask = jnp.where((slot >= first) & (slot < first + size), 1.0, 0.0)
+                first = first + size
+                outputs = outputs + mask * product[COLS * m : COLS * m + COLS, :]
+            ub[:COLS] = outputs.astype(BF16)
             ub[COLS:] = jnp.zeros((COLS, LANES), BF16)
 
         @pl.when(step > 0)
@@ -509,12 +525,9 @@
 
         @pl.when(step < ITERS)
         def _():
-            def back_part(xx, _):
-                image[:, features(xx)] = fold(dot_nt(ub[...], block_of(xx)))
+            for xx in range(4):
+                image[:, 1280 * xx : 1280 * xx + 1280] = fold(dot(ub[...], turned[xx]))
                 swap_copy(step, xx).start()
-                return 0
-
-            each(back_part)
 
         @pl.when(step == 0)
         def _():
@@ -619,6 +632,8 @@
             pltpu.VMEM((COLS, 128), F32),
             pltpu.VMEM((COLS, 128), F32),
             pltpu.VMEM((2 * COLS, LANES), BF16),
+            pltpu.VMEM((MODELS * COLS, LANES), F32),
+            pltpu.VMEM((4, LANES, 1280), BF16),
             pltpu.VMEM((32, COLS, 256), F32),
             pltpu.VMEM((16, COLS, 256), F32),
             pltpu.VMEM((32, COLS, 256), BF16),

time: 145 us -> 137 us (0.945)
  Pallas kernels: 143 us -> 135 us
    pallas_call x1, Pallas kernels: 143 us -> 135 us  [body(): pl.pallas_call(solve_kernel, out_shape=jax.ShapeDtypeStruct((160, 256), F...]
where the time goes in v4:
time: 137 us
  Pallas kernels  135 us (99%)
  local copies, waits for them, and re-layouts  1.59 us (1%)
    pallas_call x1, Pallas kernels, body(): pl.pallas_call(solve_kernel, out_shape=jax.ShapeDtypeStruct((160, 256), F...  135 us

profile of v4, /device:TPU:1, one launch (start us, length us, event | category | flops | bytes accessed | tf_op | source)
XLA Modules:
  0.0 136.8 jit_solution(12085004159573645663)
XLA Ops:
  0.0 135.2 %shard_map.46 = f32[160,256]{1,0:T(8,128)} custom-call(bf16[160,512]{1,0:T(8,128)(2,1)} %bitcast.3, f32[1,160]{1,0:T(1,128)} %g_ref.1, bf16[1280,256]{1,0:T(8,128)(2,1)} %bitcast.2, s32[8]{0:T(128)} %len_ref.1), custom_call_target="tpu_custom_call" | custom-call | tf_op jit(solution)/shard_map/pallas_call | solution.py:608
  135.2 1.6 %copy.6 = f32[160,256]{1,0:T(8,128)} copy(f32[160,256]{1,0:T(8,128)} %shard_map.46) | data formatting | bytes 327680

commit v5 on v4

--- a/solution.py
+++ b/solution.py
@@ -116,7 +116,7 @@
 
     def run(self, copies, extra):
         placed, arrival, begins = self.order()
-        extra = [(max([at] + [arrival[d] for d in deps]), deps, call) for at, deps, call in extra]
+        extra = [(at + max([arrival[d] for d in deps], default=0.0), deps, call) for at, deps, call in extra]
         extra = sorted(extra, key=lambda e: e[0])
         started, waited = {}, set()
 
@@ -238,7 +238,7 @@
 def solve_kernel(
     h_ref, g_ref, w_ref, len_ref, out_ref,
     sums, scales, halves, pieces, wt, n_ref, wbuf, d2, image, sq, other, other_sq, norm, other_norm, direction, residual,
-    merged, diagonal, squared_norm, size, ub, product, turned, blocks, landed, last_blocks, last_landed, sq_send, sq_recv,
+    merged, diagonal, squared_norm, size, weighted, ub, product, turned, blocks, landed, last_blocks, last_landed, sq_send, sq_recv,
     swap_send, swap_recv, norm_send, norm_recv, out_send, out_recv, send, recv,
 ):
     t, x, c = place()
@@ -352,11 +352,11 @@
     for k in range(1, 4):
         scaled.append(copies.start(scales.at[t], scales.at[t], line(k, core)))
         scaled.append(copies.start(scales.at[t], scales.at[t], line(k, 1 - core)))
+    send_weights()
     for k in range(1, 4):
         moved[k - 1].wait_recv()
         model = lax.rem(zl + 4 - k, 4) * 2 + core
         handed.append(copies.start(pieces.at[model], pieces.at[model], sibling))
-    send_weights()
     for copy in scaled + handed:
         copy.wait_recv()
 
@@ -380,8 +380,10 @@
         tile = jnp.where(lax.rem(lane, 8) == m, total, tile)
         return acc + dot(normed, pick), tile, first + size
 
-    zero = (jnp.zeros((80, QUART), F32), jnp.zeros((80, 128), F32), jnp.int32(0))
-    acc, tile, _ = lax.fori_loop(0, MODELS, add_model, zero)
+    carry = (jnp.zeros((80, QUART), F32), jnp.zeros((80, 128), F32), jnp.int32(0))
+    for m in range(MODELS):
+        carry = add_model(m, carry)
+    acc, tile, _ = carry
     high = tile.astype(BF16).astype(F32)
     middle = (tile - high).astype(BF16).astype(F32)
     tile = jnp.where(lane < 8, high, jnp.where(lane < 16, middle, tile - high - middle))
@@ -394,10 +396,12 @@
         return n_ref[xx].reshape(1280, LANES)
 
     def features(xx):
-        return pl.ds(pl.multiple_of(xx * 1280, 128), 1280)
+        return pl.ds(xx * 1280 if isinstance(xx, int) else pl.multiple_of(xx * 1280, 128), 1280)
 
     def each(body, init=0):
-        return lax.fori_loop(0, 4, body, init)
+        for xx in range(4):
+            init = body(xx, init)
+        return init
 
     def fold_lanes(v):
         return functools.reduce(jnp.add, [v[:, 128 * k : 128 * k + 128] for k in range(10)])
@@ -430,21 +434,17 @@
     take = (lax.rem(take, 8) == lax.broadcasted_iota(jnp.int32, (16, 128), 0)) & (take < 24)
     take = jnp.where(take, 1.0, 0.0).astype(BF16)
 
-    def use_block(k):
+    def use_block(k, step):
         xx = lax.rem(x + k + 4, 4)
-        spare = n_ref[xx, :, :, :, :, :, LANES - 128 :].reshape(1280, 128)
-        sq[:, features(xx)] = dot_nt(take, spare)[:MODELS]
+        if step == 0:
+            spare = n_ref[xx, :, :, :, :, :, LANES - 128 :].reshape(1280, 128)
+            sq[:, features(xx)] = dot_nt(take, spare)[:MODELS]
         weights = wbuf[:, :, features(xx)].reshape(MODELS * COLS, 1280)
-
-        def part(step, _):
-            at = pl.ds(pl.multiple_of(step * CHUNK, CHUNK), CHUNK)
-            block = n_ref[xx, :, :, :, :, :, at].reshape(1280, CHUNK)
-            turned[xx, at, :] = block.T
-            more = dot(weights, block)
-            product[:, at] = more if k == 0 else product[:, at] + more
-            return 0
-
-        lax.fori_loop(0, LANES // CHUNK, part, 0)
+        at = slice(CHUNK * step, CHUNK * step + CHUNK)
+        block = n_ref[xx, :, :, :, :, :, at].reshape(1280, CHUNK)
+        turned[xx, at, :] = block.T
+        more = dot(weights, block)
+        product[:, at] = more if k == 0 else product[:, at] + more
 
     def wait_weights():
         for copy in w_handed:
@@ -452,7 +452,8 @@
 
     plan, whole = gather_plan(n_ref, t, x, c)
     first = [(8.0, [], hand_weights), (0.0, whole[0], wait_weights)]
-    sent = plan.run(copies, first + [(0.0, whole[k], functools.partial(use_block, k)) for k in (0, 1, -1, 2)])
+    uses = [(1.0 * i, whole[k], functools.partial(use_block, k, i)) for k in (0, 1, -1, 2) for i in range(5)]
+    sent = plan.run(copies, first + uses)
     sent += moved + handed + scaled
     swap_sq = copies.start(sq, other_sq, sibling)
 
@@ -467,7 +468,8 @@
         direction[:, part] = right
         residual[:, part] = right
         d2[:, part] = split(right)
-        return total + fold_lanes(right * right)
+        length, inner = total
+        return length + fold_lanes(right * right), inner + fold_lanes(diagonal[0:1, part] * right * right)
 
     def spread_out(v):
         return jnp.broadcast_to(jnp.sum(v, axis=1, keepdims=True), (COLS, 128))
@@ -525,25 +527,24 @@
 
         @pl.when(step < ITERS)
         def _():
-            for xx in range(4):
-                image[:, 1280 * xx : 1280 * xx + 1280] = fold(dot(ub[...], turned[xx]))
-                swap_copy(step, xx).start()
+            for xx in range(5):
+                if xx < 4:
+                    image[:, 1280 * xx : 1280 * xx + 1280] = fold(dot(ub[...], turned[xx]))
+                if xx > 0:
+                    swap_copy(step, xx - 1).start()
 
         @pl.when(step == 0)
         def _():
             swap_sq.wait()
-            squared_norm[...] = spread_out(each(right_part, jnp.zeros((COLS, 128), F32)))
+            zero = jnp.zeros((COLS, 128), F32)
+            length, inner = each(right_part, (zero, zero))
+            squared_norm[...], weighted[...] = spread_out(length), spread_out(inner)
             merged[...] = jnp.zeros_like(merged)
 
         @pl.when(step > 0)
         def _():
-            def weighted(xx, total):
-                now = direction[:, features(xx)]
-                return total + fold_lanes(diagonal[0:1, features(xx)] * now * now)
-
-            inner = spread_out(each(weighted, jnp.zeros((COLS, 128), F32)))
             norm_copy(step).wait()
-            curvature = MIXING * (norm[step] + other_norm[step]) + inner
+            curvature = MIXING * (norm[step] + other_norm[step]) + weighted[...]
             size[...] = squared_norm[...] / curvature
 
         @pl.when((step > 0) & (step < ITERS))
@@ -567,14 +568,14 @@
             ratio = (norm_next / squared_norm[...])[:, :1]
             squared_norm[...] = norm_next
 
-            def direction_part(xx, _):
+            def direction_part(xx, total):
                 part = features(xx)
                 now = residual[:, part] + ratio * direction[:, part]
                 direction[:, part] = now
                 d2[:, part] = split(now)
-                return 0
-
-            each(direction_part)
+                return total + fold_lanes(diagonal[0:1, part] * now * now)
+
+            weighted[...] = spread_out(each(direction_part, jnp.zeros((COLS, 128), F32)))
 
         @pl.when(step < ITERS)
         def _():
@@ -589,6 +590,9 @@
     lax.fori_loop(0, ITERS + 1, solve_step, 0)
     send_blocks(lambda part: size[:, :1] * direction[:, part], last_blocks, last_landed, 16)
 
+    for copy in sent + w_moved + w_handed:
+        copy.wait_send()
+
     def wait_blocks(k, _):
         block_copy(k, blocks, landed, 0).wait()
         block_copy(k, last_blocks, last_landed, 16).wait()
@@ -597,8 +601,6 @@
     lax.fori_loop(1, 16, wait_blocks, 0)
     result = landed[...] + last_landed[...].astype(F32)
     out_ref[...] = result.reshape(256, 256).T[:160]
-    for copy in sent + w_moved + w_handed:
-        copy.wait_send()
 
 
 def body(hidden, gains, weights, lengths):
@@ -631,6 +633,7 @@
             pltpu.VMEM((8, WIDTH), F32),
             pltpu.VMEM((COLS, 128), F32),
             pltpu.VMEM((COLS, 128), F32),
+            pltpu.VMEM((COLS, 128), F32),
             pltpu.VMEM((2 * COLS, LANES), BF16),
             pltpu.VMEM((MODELS * COLS, LANES), F32),
             pltpu.VMEM((4, LANES, 1280), BF16),

time: 137 us -> 134 us (0.978)
  Pallas kernels: 135 us -> 132 us
    pallas_call x1, Pallas kernels: 135 us -> 132 us  [body(): pl.pallas_call(solve_kernel, out_shape=jax.ShapeDtypeStruct((160, 256), F...]
where the time goes in v5:
time: 134 us
  Pallas kernels  132 us (99%)
  local copies, waits for them, and re-layouts  1.59 us (1%)
    pallas_call x1, Pallas kernels, body(): pl.pallas_call(solve_kernel, out_shape=jax.ShapeDtypeStruct((160, 256), F...  132 us

profile of v5, /device:TPU:1, one launch (start us, length us, event | category | flops | bytes accessed | tf_op | source)
XLA Modules:
  0.0 133.8 jit_solution(14126508941406223470)
XLA Ops:
  0.0 132.2 %shard_map.46 = f32[160,256]{1,0:T(8,128)} custom-call(bf16[160,512]{1,0:T(8,128)(2,1)} %bitcast.3, f32[1,160]{1,0:T(1,128)} %g_ref.1, bf16[1280,256]{1,0:T(8,128)(2,1)} %bitcast.2, s32[8]{0:T(128)} %len_ref.1), custom_call_target="tpu_custom_call" | custom-call | tf_op jit(solution)/shard_map/pallas_call | solution.py:610
  132.2 1.6 %copy.6 = f32[160,256]{1,0:T(8,128)} copy(f32[160,256]{1,0:T(8,128)} %shard_map.46) | data formatting | bytes 327680

commit v6 on v5

--- a/solution.py
+++ b/solution.py
@@ -55,7 +55,7 @@
 
 
 class Plan:
-    RATE, HOP = 45e3, 2.3
+    RATE, HOP = 42e3, 3.0
 
     def __init__(self):
         self.tasks, self.level = [], []
@@ -308,7 +308,11 @@
         return 0
 
     def wait_sums(k, _):
-        sums_copy(k).wait()
+        sums_copy(k).wait_recv()
+        return 0
+
+    def wait_sums_sent(k, _):
+        sums_copy(k).wait_send()
         return 0
 
     lax.fori_loop(1, 32, send_sums, 0)
@@ -487,17 +491,14 @@
         )
 
     def send_blocks(values, source, target, first):
-        def cut(group, _):
-            value = values(pl.ds(pl.multiple_of(group * 640, 128), 640))
-            for k in range(4):
-                source[group * 4 + k, :, 0:160] = value[:, 160 * k : 160 * k + 160].astype(source.dtype)
-            return 0
-
         def send_one(k, _):
             block_copy(k, source, target, first).start()
             return 0
 
-        lax.fori_loop(0, 8, cut, 0)
+        for group in range(8):
+            value = values(pl.ds(640 * group, 640))
+            for k in range(4):
+                source[group * 4 + k, :, 0:160] = value[:, 160 * k : 160 * k + 160].astype(source.dtype)
         target[chip] = source[x * 8 + t]
         lax.fori_loop(1, 16, send_one, 0)
 
@@ -592,6 +593,7 @@
 
     for copy in sent + w_moved + w_handed:
         copy.wait_send()
+    lax.fori_loop(1, 32, wait_sums_sent, 0)
 
     def wait_blocks(k, _):
         block_copy(k, blocks, landed, 0).wait()

time: 134 us -> 133 us (level)
  no operation moved by 1% of the time
where the time goes in v6:
time: 133 us
  Pallas kernels  132 us (99%)
  local copies, waits for them, and re-layouts  1.59 us (1%)
    pallas_call x1, Pallas kernels, body(): pl.pallas_call(solve_kernel, out_shape=jax.ShapeDtypeStruct((160, 256), F...  132 us

profile of v6, /device:TPU:1, one launch (start us, length us, event | category | flops | bytes accessed | tf_op | source)
XLA Modules:
  0.0 133.2 jit_solution(17698234218701874470)
XLA Ops:
  0.0 131.6 %shard_map.46 = f32[160,256]{1,0:T(8,128)} custom-call(bf16[160,512]{1,0:T(8,128)(2,1)} %bitcast.3, f32[1,160]{1,0:T(1,128)} %g_ref.1, bf16[1280,256]{1,0:T(8,128)(2,1)} %bitcast.2, s32[8]{0:T(128)} %len_ref.1), custom_call_target="tpu_custom_call" | custom-call | tf_op jit(solution)/shard_map/pallas_call | solution.py:612
  131.6 1.6 %copy.6 = f32[160,256]{1,0:T(8,128)} copy(f32[160,256]{1,0:T(8,128)} %shard_map.46) | data formatting | bytes 327680
